TPU v7x, 32 devices: a whole 2x2x4 slice. The times are simulated.
32 devices in a mesh: slide: 8 (over z, core), tile: 4 (over y, x).
Axes of the slice: x: 2, y: 2, z: 4, core: 2. Of those that a mesh axis runs over, the one named last changes fastest.
Arguments:
- features: bfloat16 [8, 4, 32, 32, 768], P('slide', 'tile'), may hold values from -6 to 6
- cotangent: bfloat16 [8, 4, 32, 32, 768], P('slide', 'tile'), may hold values from -0.59765625 to 0.59765625
- neighbours: int32 [8, 4, 8], P('slide'), may hold values from 0 to 4, as said below
- skip_flags: int32 [1, 8], P(None, 'slide'), may hold values 0 or 1
- dw_weight: float32 [1, 7, 7, 768], replicated, may hold values from -0.875 to 0.875
- ln_gain: float32 [1, 768], replicated, may hold values from 0.5 to 1.5
- ln_bias: float32 [1, 768], replicated, may hold values from -3 to 3
- up_weight: bfloat16 [1, 3072, 768], replicated, may hold values from -0.21875 to 0.21875
- up_bias: float32 [1, 3072], replicated, may hold values from -3 to 3
- down_weight: bfloat16 [1, 768, 3072], replicated, may hold values from -0.109375 to 0.109375
- down_bias: float32 [1, 768], replicated, may hold values from -3 to 3
- layer_scale: float32 [1, 768], replicated, may hold values from 0.5 to 1.5
Outputs:
- block_out: bfloat16 [8, 4, 32, 32, 768], P('slide', 'tile')
- input_grad: bfloat16 [8, 4, 32, 32, 768], P('slide', 'tile')
- weight_grads: float32 [1, 3072, 1536], P(None, ('slide', 'tile'))
- kernel_grads: float32 [1, 7, 7, 768], replicated
- channel_grads: float32 [1, 4, 768], replicated
- bias_grads: float32 [1, 3072], replicated
Inputs may be any that keep to these rules, and one draw needn't show every extreme that they name: neighbours[s, a, d] is the tile of slide s next to tile a in direction d, or 4 where no tissue tile lies there; tiles of a slide sit on a grid four tiles wide, and b is a's neighbour in one direction exactly when a is b's in the opposite direction.
All inputs are finite; a program needn't handle non-finite values. No bound on the sum of `skip_flags` on one device may be relied on, other than what follows from the above.
Results may differ from a plain program's by a relative error of at most 0.015.
Values may be sent and summed in bfloat16 or wider, within the bound.
A program may use at most 192 MiB of HBM per device.

v0:
```python
import jax
import jax.numpy as jnp
from jax import lax
from jax.sharding import PartitionSpec as P

ln_eps = 1e-06
root_half = 0.7071067811865476
inv_root_two_pi = 0.3989422804014327
conv_dims = ("NHWC", "HWIO", "NHWC")


def border_rows(tiles):
    return jnp.stack([tiles[:, :3], tiles[:, -3:]], 1)


def border_columns(tiles):
    return jnp.stack([tiles[:, :, :3], tiles[:, :, -3:]], 1)


def extend(tiles, row_strips, column_strips, table_rows):
    row_strips = jnp.concatenate([row_strips, jnp.zeros_like(row_strips[:1])], 0)
    column_strips = jnp.concatenate([column_strips, jnp.zeros_like(column_strips[:1])], 0)
    north = row_strips[table_rows[:, 0], 1]
    south = row_strips[table_rows[:, 1], 0]
    west = column_strips[table_rows[:, 2], 1]
    east = column_strips[table_rows[:, 3], 0]
    north_west = row_strips[table_rows[:, 4], 1][:, :, -3:]
    north_east = row_strips[table_rows[:, 5], 1][:, :, :3]
    south_west = row_strips[table_rows[:, 6], 0][:, :, -3:]
    south_east = row_strips[table_rows[:, 7], 0][:, :, :3]
    upper = jnp.concatenate([north_west, north, north_east], 2)
    middle = jnp.concatenate([west, tiles, east], 2)
    lower = jnp.concatenate([south_west, south, south_east], 2)
    return jnp.concatenate([upper, middle, lower], 1)


def depthwise(extended, kernel):
    channels = kernel.shape[-1]
    return lax.conv_general_dilated(
        extended,
        kernel[:, :, None, :],
        (1, 1),
        "VALID",
        dimension_numbers=conv_dims,
        feature_group_count=channels,
        precision=lax.Precision.HIGHEST,
    )


def kernel_grad(extended, conv_grad):
    channels = conv_grad.shape[-1]
    total = jnp.zeros((7, 7, channels), jnp.float32)
    kernel = jnp.transpose(conv_grad, (1, 2, 0, 3))
    single = lax.conv_general_dilated(
        extended,
        kernel,
        (1, 1),
        "VALID",
        dimension_numbers=conv_dims,
        feature_group_count=channels,
        precision=lax.Precision.HIGHEST,
    )
    total = total + single[0]
    return total


def normalize(values):
    average = jnp.mean(values, axis=-1, keepdims=True)
    centred = values - average
    inv_std = lax.rsqrt(jnp.mean(centred * centred, axis=-1, keepdims=True) + ln_eps)
    return (centred * inv_std, inv_std)


def gelu_parts(pre):
    cdf = 0.5 * (1.0 + lax.erf(pre * root_half))
    return (cdf, cdf + pre * inv_root_two_pi * jnp.exp(-0.5 * pre * pre))


def contract(left, right):
    return lax.dot_general(
        left, right, (((1,), (1,)), ((), ())), preferred_element_type=jnp.float32
    )


def over_pixels(left, right):
    return lax.dot_general(
        left, right, (((0,), (0,)), ((), ())), preferred_element_type=jnp.float32
    )


def mlp_forward(flat, up_matrix, up_shift, down_matrix, down_shift):
    pre = contract(flat, up_matrix) + up_shift
    cdf, slope = gelu_parts(pre)
    act = (pre * cdf).astype(jnp.bfloat16)
    branch = contract(act, down_matrix) + down_shift
    return (pre, act, branch)


def mlp_backward(grad_flat, branch_factor, whitened, inv_std, pre, up_matrix, down_matrix, gain):
    branch_grad = (branch_factor * grad_flat).astype(jnp.bfloat16)
    act_grad = jnp.dot(branch_grad, down_matrix, preferred_element_type=jnp.float32)
    cdf, slope = gelu_parts(pre)
    pre_grad = (act_grad * slope).astype(jnp.bfloat16)
    normed_grad = jnp.dot(pre_grad, up_matrix, preferred_element_type=jnp.float32)
    scaled = normed_grad * gain
    conv_grad = inv_std * (
        scaled
        - jnp.mean(scaled, axis=-1, keepdims=True)
        - whitened * jnp.mean(scaled * whitened, axis=-1, keepdims=True)
    )
    sums = jnp.stack(
        [
            jnp.sum(normed_grad * whitened, axis=0),
            jnp.sum(normed_grad, axis=0),
            jnp.sum(branch_grad.astype(jnp.float32), axis=0),
        ]
    )
    return (
        branch_grad,
        pre_grad,
        conv_grad.astype(jnp.bfloat16),
        sums,
        jnp.sum(pre_grad.astype(jnp.float32), axis=0),
    )


def on_device(
    features,
    cotangent,
    neighbours,
    skip_flags,
    dw_weight,
    ln_gain,
    ln_bias,
    up_weight,
    up_bias,
    down_weight,
    down_bias,
    layer_scale,
):
    tile_count = features.shape[1]
    channels = features.shape[4]
    blocks = dw_weight.shape[0]
    hidden_units = up_weight.shape[1]
    tile_shape = features.shape[1:]
    first_tile = lax.axis_index("tile") * tile_count
    table_rows = lax.dynamic_slice_in_dim(neighbours[0], first_tile, tile_count, 0)
    current = features[0]
    layer = 0
    keep = (1 - skip_flags[layer, 0]).astype(jnp.float32)
    row_strips = lax.all_gather(border_rows(current), "tile", axis=0, tiled=True)
    column_strips = lax.all_gather(border_columns(current), "tile", axis=0, tiled=True)
    extended = extend(current, row_strips, column_strips, table_rows).astype(jnp.float32)
    conv = depthwise(extended, dw_weight[layer])
    whitened, inv_std = normalize(conv.reshape(-1, channels))
    flat = (whitened * ln_gain[layer] + ln_bias[layer]).astype(jnp.bfloat16)
    pre, act, branch = mlp_forward(
        flat, up_weight[layer], up_bias[layer], down_weight[layer], down_bias[layer]
    )
    output = (
        current.astype(jnp.float32).reshape(-1, channels) + keep * layer_scale[layer] * branch
    ).astype(jnp.bfloat16)
    saved = [(extended, whitened, inv_std, flat, pre, act, branch, keep)]
    current = output.reshape(tile_shape)
    step_grad = cotangent[0]
    weight_list = []
    kernel_list = []
    channel_list = []
    bias_list = []
    for layer in reversed(range(blocks)):
        extended, whitened, inv_std, flat, pre, act, branch, keep = saved[layer]
        grad_flat = step_grad.astype(jnp.float32).reshape(-1, channels)
        scale_grad = jnp.sum(grad_flat * keep * branch, axis=0)
        branch_factor = keep * layer_scale[layer]
        branch_grad, pre_grad, conv_grad, sums, up_bias_sum = mlp_backward(
            grad_flat,
            branch_factor,
            whitened,
            inv_std,
            pre,
            up_weight[layer],
            down_weight[layer],
            ln_gain[layer],
        )
        first_row = jnp.int32(0)
        pre_rows = lax.dynamic_slice_in_dim(
            pre_grad,
            first_row,
            hidden_units // lax.axis_size(("slide", "tile")) * lax.axis_size(("slide", "tile")),
            1,
        )
        act_rows = lax.dynamic_slice_in_dim(
            act,
            first_row,
            hidden_units // lax.axis_size(("slide", "tile")) * lax.axis_size(("slide", "tile")),
            1,
        )
        weight_rows = lax.psum_scatter(
            jnp.concatenate([over_pixels(pre_rows, flat), over_pixels(act_rows, branch_grad)], 1),
            ("slide", "tile"),
            scatter_dimension=0,
            tiled=True,
        )
        conv_tiles = conv_grad.reshape(tile_shape)
        grad_rows, grad_columns = (
            lax.all_gather(border_rows(conv_tiles), "tile", axis=0, tiled=True),
            lax.all_gather(border_columns(conv_tiles), "tile", axis=0, tiled=True),
        )
        kernel_sum = kernel_grad(extended, conv_tiles.astype(jnp.float32))
        channel_sum = jnp.concatenate([sums, scale_grad[None]], 0)
        kernel_total, channel_total, bias_total = lax.psum(
            (kernel_sum, channel_sum, up_bias_sum), ("slide", "tile")
        )
        grad_extended = extend(conv_tiles, grad_rows, grad_columns, table_rows).astype(jnp.float32)
        back = depthwise(grad_extended, dw_weight[layer][::-1, ::-1])
        step_grad = (step_grad.astype(jnp.float32) + back).astype(jnp.bfloat16)
        weight_list.append(weight_rows)
        kernel_list.append(kernel_total)
        channel_list.append(channel_total)
        bias_list.append(bias_total)
    weight_grads = jnp.stack(weight_list[::-1])
    kernel_grads = jnp.stack(kernel_list[::-1])
    channel_grads = jnp.stack(channel_list[::-1])
    bias_grads = jnp.stack(bias_list[::-1])
    return (current[None], step_grad[None], weight_grads, kernel_grads, channel_grads, bias_grads)


def solution(mesh):
    return jax.shard_map(
        on_device,
        mesh=mesh,
        in_specs=(
            P("slide", "tile", None, None, None),
            P("slide", "tile", None, None, None),
            P("slide", None, None),
            P(None, "slide"),
            P(),
            P(),
            P(),
            P(),
            P(),
            P(),
            P(),
            P(),
        ),
        out_specs=(
            P("slide", "tile", None, None, None),
            P("slide", "tile", None, None, None),
            P(None, ("slide", "tile"), None),
            P(),
            P(),
            P(),
        ),
        check_vma=False,
    )
```

profile of v0, /device:TPU:0, one launch (start us, length us, event | category | flops | bytes accessed | tf_op | source)
XLA Modules:
  0.0 631.9 jit_solution(15251268330595976069)
XLA Ops:
  7.2 1.0 slice_bitcast_fusion.7
  8.2 0.7 pad_maximum_fusion.3
  9.0 0.0 all-gather.7.cloned.1.call-start
  9.1 1.3 slice_bitcast_fusion.3
  10.4 0.3 pad_maximum_fusion.1
  10.6 0.7 copy.58
  11.5 0.7 fusion.61
  22.0 4.5 copy.60
  27.3 3.8 copy_convert_fusion
  31.2 2.0 copy.87
  33.2 5.9 convert_reduce_fusion.1
  39.1 1.5 copy.83
  45.5 1.2 fusion.43
  46.9 0.6 copy.91
  47.5 0.2 copy.55
  47.8 0.9 copy.64
  48.7 22.3 %all-gather.7.cloned.1.call-done = bf16[4,2,32,3,768]{4,2,3,1,0:T(8,128)(2,1)} async-done(((bf16[1,2,32,3,768]{4,2,3,1,0:T(8,128)(2,1)}), bf16[4,2,32,3,768]{4,2,3,1,0:T(8,128)(2,1)}) %all-gather.7.cloned.1.call-update) | async-done | bytes 1179664 | tf_op jit(solution)/shard_map/all_gather | solution.py:152
  71.1 1.0 fusion.55
  72.0 0.6 copy.59
  72.6 0.2 copy.61
  72.9 24.0 %maximum_maximum_fusion = bf16[1,38,38,768]{3,0,2,1:T(2,128)(2,1)S(1)} fusion(bf16[1,3,3,768]{3,0,2,1:T(2,128)(2,1)} %copy.91, bf16[1,3,32,768]{3,0,2,1:T(2,128)(2,1)} %copy.64, bf16[1,3,3,768]{3,0,2,1:T(2,128)(2,1)S(1)} %copy.90, bf16[1,32,3,768]{3,0,2,1:T(2,128)(2,1)S(1)} %copy.61, bf16[1,32,32,768]{3,0,2,1:T(2,128)(2,1)S(1)} %copy.60, ...), kind=kLoop, calls=%fused_computation.17 | loop fusion | flops 8871936 | bytes 4435968 | tf_op jit(solution)/shard_map/concatenate | solution.py:34
  96.9 71.6 %fusion.62 = (f32[32,32]{1,0:T(8,128)S(1)}, f32[1,32,32,768]{3,0,2,1:T(1,128)S(1)}) fusion(bf16[1,38,38,768]{3,0,2,1:T(2,128)(2,1)S(1)} %maximum_maximum_fusion, f32[1,7,7,768]{3,0,2,1:T(1,128)S(1)} %copy-done.11), kind=kOutput, calls=%fused_computation.118 | convolution fusion | flops 463207424 | bytes 5518336 | tf_op jit(solution)/shard_map/conv_general_dilated | solution.py:39
  168.6 0.1 div.17
  168.7 16.0 %multiply_reduce_fusion.2 = f32[32,32]{1,0:T(8,128)S(1)} fusion(f32[1,32,32,768]{3,0,2,1:T(1,128)S(1)} %get-tuple-element.245, f32[32,32]{1,0:T(8,128)S(1)} %broadcast_multiply_fusion), kind=kLoop, calls=%fused_computation.57 | loop fusion | flops 2358272 | bytes 3153920 | tf_op jit(solution)/shard_map/reduce_sum | solution.py:70
  184.7 2.0 copy.84
  186.7 0.1 rsqrt.13
  186.8 5.2 add_convert_fusion.1
  192.1 0.4 copy.82
  192.4 0.3 copy-done.18
  192.7 9.6 %multiply_convert_fusion = (bf16[1024,3072]{1,0:T(8,128)(2,1)}, f32[1024,3072]{1,0:T(8,128)S(1)}) fusion(f32[3072]{0:T(1024)S(1)} %bitcast.167, bf16[1024,768]{1,0:T(8,128)(2,1)S(1)} %bitcast.159, bf16[1,3072,768]{2,1,0:T(8,128)(2,1)} %param.19), kind=kOutput, calls=%fused_computation.8 | convolution fusion | flops 4850712576 | bytes 25178112 | tf_op jit(solution)/shard_map/dot_general | solution.py:80
  202.4 12.3 %convert_reduce_fusion = (f32[3072]{0:T(1024)S(1)}, bf16[1024,3072]{1,0:T(8,128)(2,1)}) fusion(f32[1024,3072]{1,0:T(8,128)S(1)} %get-tuple-element.247, f32[3072]{0:T(1024)S(1)} %bitcast.168, bf16[1024,768]{1,0:T(8,128)(2,1)S(1)} %bitcast.157, bf16[1,768,3072]{2,1,0:T(8,128)(2,1)S(1)} %bitcast.166), kind=kOutput, calls=%fused_computation.7 | convolution fusion | flops 4872729600 | bytes 25190400 | tf_op jit(solution)/shard_map/dot_general | solution.py:101
  214.7 8.9 %multiply_reduce_fusion = (f32[768]{0:T(1024)S(1)}, f32[1024]{0:T(1024)S(1)}, f32[1024]{0:T(1024)S(1)}, f32[768]{0:T(1024)S(1)}, bf16[1024,768]{1,0:T(8,128)(2,1)}, /*index=5*/f32[1024,768]{1,0:T(8,128)S(1)}) fusion(f32[1,32,32,768]{3,2,0,1:T(8,128)S(1)} %copy-done.2, f32[1024]{0:T(1024)S(1)} %div.17, f32[1024]{0:T(1024)S(1)} %rsqrt.13, ...), kind=kOutput, calls=%fused_computation.51 | convolution fusion | flops 4841271296 | bytes 18903040 | tf_op jit(solution)/shard_map/dot_general | solution.py:104
  223.6 1.3 multiply_convert_fusion.1
  224.9 1.2 copy-done.4
  226.1 0.2 slice_bitcast_fusion.1
  226.3 0.7 pad_maximum_fusion.4
  227.1 10.8 %fusion.32 = (f32[768]{0:T(1024)S(1)}, bf16[1024,768]{1,0:T(8,128)(2,1)}, bf16[1024,768]{1,0:T(8,128)(2,1)}) fusion(f32[1,1,32,32,768]{4,3,0,2,1:T(8,128)} %copy.87, f32[]{:T(128)} %bitcast.1, f32[768]{0:T(1024)S(1)} %reduce.6, f32[768]{0:T(1024)S(1)} %multiply_reduce_fusion.4, bf16[1,1,32,32,768]{4,3,2,1,0:T(8,128)(2,1)S(1)} %copy-done.8, ...), kind=kOutput, calls=%fused_computation.40 | convolution fusion | flops 4839701504 | bytes 18883588 | tf_op jit(solution)/shard_map/dot_general | solution.py:80
  237.8 0.3 pad_maximum_fusion.2
  238.1 0.7 copy.69
  238.9 10.1 %fusion.64 = f32[3072,768]{0,1:T(8,128)} fusion(bf16[1024,3072]{1,0:T(8,128)(2,1)} %get-tuple-element.246, bf16[1024,768]{1,0:T(8,128)(2,1)} %get-tuple-element.211), kind=kOutput, calls=%fused_computation.120 | convolution fusion | flops 4831838208 | bytes 17301504 | tf_op jit(solution)/shard_map/dot_general | solution.py:86
  249.0 0.0 reduce-scatter.4.cloned.1.call-start
  249.0 7.4 %fusion.63 = f32[3072,768]{0,1:T(8,128)S(1)} fusion(bf16[1024,3072]{1,0:T(8,128)(2,1)} %get-tuple-element.250, bf16[1024,768]{1,0:T(8,128)(2,1)S(1)} %copy-done.19), kind=kOutput, calls=%fused_computation.119 | convolution fusion | flops 4831838208 | bytes 17301504 | tf_op jit(solution)/shard_map/dot_general | solution.py:86
  256.5 7.1 %pad_maximum_fusion = f32[3072,1536]{0,1:T(8,128)} fusion(f32[3072,768]{0,1:T(8,128)S(1)} %copy-done.3, f32[3072,768]{0,1:T(8,128)S(1)} %fusion.63), kind=kLoop, calls=%fused_computation.1 | loop fusion | flops 4718592 | bytes 37748736 | tf_op jit(solution)/shard_map/concatenate | solution.py:199
  263.6 18.7 %copy.80 = f32[3072,1536]{1,0:T(8,128)} copy(f32[3072,1536]{0,1:T(8,128)} %pad_maximum_fusion) | data formatting | bytes 37748736
  282.3 0.8 copy-done.12
  283.2 1.9 rev.3
  285.1 4.5 copy.71
  289.7 40.2 %all-reduce.4 = (f32[1,4,768]{2,1,0:T(4,128)}, f32[1,3072]{1,0:T(1,128)}) all-reduce(f32[1,4,768]{2,1,0:T(4,128)S(1)} %maximum_bitcast_fusion, f32[1,3072]{1,0:T(1,128)S(1)} %bitcast.162), channel_id=1, replica_groups=mesh['slide'=8,'tile'=4] {'slide','tile'}, use_global_device_ids=true, to_apply=%region_10.0 | all-reduce | flops 6144 | bytes 49152 | tf_op jit(solution)/shard_map/psum | solution.py:211
  330.0 32.8 %fusion.36 = f32[1,7,7,768]{3,0,2,1:T(1,128)} fusion(bf16[1,38,38,768]{3,0,2,1:T(2,128)(2,1)} %copy-done.7, bf16[32,32,1,768]{3,1,0,2:T(8,128)(2,1)} %bitcast.152), kind=kOutput, calls=%fused_computation.47 | convolution fusion | flops 77070336 | bytes 3941376 | tf_op jit(solution)/shard_map/conv_general_dilated | solution.py:54
  362.8 1.2 fusion.49
  364.2 0.6 copy.95
  364.8 0.2 copy.68
  365.0 0.9 copy.75
  366.0 1.0 fusion.57
  366.9 0.2 copy.70
  367.2 0.2 copy.72
  367.4 24.0 %fusion.78 = bf16[1,38,38,768]{3,0,2,1:T(2,128)(2,1)S(1)} fusion(bf16[1,3,3,768]{3,0,2,1:T(2,128)(2,1)} %copy.95, bf16[1,3,32,768]{3,0,2,1:T(2,128)(2,1)} %copy.75, bf16[1,3,3,768]{3,0,2,1:T(2,128)(2,1)S(1)} %copy.94, bf16[1,32,3,768]{3,0,2,1:T(2,128)(2,1)S(1)} %copy.72, bf16[1,32,32,768]{3,0,2,1:T(2,128)(2,1)S(1)} %copy.71, ...), kind=kLoop, calls=%fused_computation.19.clone.clone.clone.1 | loop fusion | flops 8871936 | bytes 4435968 | tf_op jit(solution)/shard_map/conv_general_dilated | solution.py:39
  391.5 30.4 %fusion.35 = bf16[1,32,32,768]{3,0,2,1:T(2,128)(2,1)S(1)} fusion(f32[7,7,1,768]{3,1,0,2:T(8,128)S(1)} %bitcast.161, bf16[1,1,32,32,768]{4,3,2,1,0:T(8,128)(2,1)S(1)} %copy-done.6, bf16[1,38,38,768]{3,0,2,1:T(2,128)(2,1)S(1)} %fusion.78), kind=kOutput, calls=%fused_computation.46 | convolution fusion | flops 464781312 | bytes 5514240 | tf_op jit(solution)/shard_map/conv_general_dilated | solution.py:39
  421.9 1.5 copy.110
  423.5 73.8 %reduce-scatter.4.cloned.1.call-done = f32[96,1536]{1,0:T(8,128)} async-done(((f32[3072,1536]{1,0:T(8,128)}), f32[96,1536]{1,0:T(8,128)}) %reduce-scatter.4.cloned.1.call-update) | async-done | bytes 589840
  497.3 1.3 copy.81
  498.6 1.1 copy.78
  499.7 123.6 %all-reduce.7.cloned.1.call-done = f32[1,7,7,768]{3,0,2,1:T(1,128)} async-done(((f32[1,7,7,768]{3,0,2,1:T(1,128)}), f32[1,7,7,768]{3,0,2,1:T(1,128)}) %all-reduce.7.cloned.1.call-update) | async-done | bytes 150544 | tf_op jit(solution)/shard_map/psum | solution.py:211
  623.3 1.6 copy.114
  (89 shorter events, 0.8 us)
Async XLA Ops:
  7.2 4.3 copy-start
  7.2 38.4 %all-gather.5.cloned.1.call-start = ((), (), s32[]{:S(2)}) async-start(), calls=%async_computation.1 | async-start | bytes 1474560 | tf_op jit(solution)/shard_map/all_gather | solution.py:151
  9.0 62.1 %all-gather.7.cloned.1.call-start = ((), (), s32[]{:S(2)}) async-start(), calls=%async_computation.2 | async-start | bytes 1474560 | tf_op jit(solution)/shard_map/all_gather | solution.py:152
  10.3 16.9 %copy-start.14 = (f32[1,768]{1,0:T(1,128)S(1)}, f32[1,768]{1,0:T(1,128)}, u32[]{:S(2)}) copy-start(f32[1,768]{1,0:T(1,128)} %param.17) | copy-start | bytes 9220
  10.3 16.9 %copy-start.15 = (f32[1,768]{1,0:T(1,128)S(1)}, f32[1,768]{1,0:T(1,128)}, u32[]{:S(2)}) copy-start(f32[1,768]{1,0:T(1,128)} %param.18) | copy-start | bytes 9220
  10.4 17.0 %copy-start.16 = (f32[1,768]{1,0:T(1,128)S(1)}, f32[1,768]{1,0:T(1,128)}, u32[]{:S(2)}) copy-start(f32[1,768]{1,0:T(1,128)} %param.22) | copy-start | bytes 9220
  11.4 351.4 %all-gather.9.cloned.1.call-start = ((), (), s32[]{:S(2)}) async-start(), calls=%async_computation.3 | async-start | bytes 1474560 | tf_op jit(solution)/shard_map/all_gather | solution.py:206
  31.2 2.0 copy-start.17
  31.2 2.0 copy-start.5
  72.8 24.1 %copy-start.11 = (f32[1,7,7,768]{3,0,2,1:T(1,128)S(1)}, f32[1,7,7,768]{3,0,2,1:T(1,128)}, u32[]{:S(2)}) copy-start(f32[1,7,7,768]{3,0,2,1:T(1,128)} %param.16) | copy-start | bytes 451588
  96.9 71.7 %copy-start.7 = (bf16[1,38,38,768]{3,0,2,1:T(2,128)(2,1)}, bf16[1,38,38,768]{3,0,2,1:T(2,128)(2,1)S(1)}, u32[]{:S(2)}) copy-start(bf16[1,38,38,768]{3,0,2,1:T(2,128)(2,1)S(1)} %maximum_maximum_fusion) | copy-start | bytes 6653956
  192.0 0.7 copy-start.18
  192.0 10.3 %slice-start.2 = ((s8[4718592]{0:T(1024)(128)(4,1)}), s8[4194304]{0:T(1024)(128)(4,1)S(1)}, s32[]{:S(2)}) async-start(s8[4718592]{0:T(1024)(128)(4,1)} %bitcast.165), calls=%async_computation.9 | async-start | bytes 8388608
  192.7 9.6 %copy-start.9 = (bf16[1,1,32,32,768]{4,3,0,2,1:T(8,128)(2,1)S(1)}, bf16[1,1,32,32,768]{4,3,0,2,1:T(8,128)(2,1)}, u32[]{:S(2)}) copy-start(bf16[1,1,32,32,768]{4,3,0,2,1:T(8,128)(2,1)} %copy.83) | copy-start | bytes 4718596
  192.7 9.6 %slice-start.3 = ((s8[4718592]{0:T(1024)(128)(4,1)}), s8[524288]{0:T(1024)(128)(4,1)S(1)}, s32[]{:S(2)}) async-start(s8[4718592]{0:T(1024)(128)(4,1)} %bitcast.165), calls=%async_computation.10 | async-start | bytes 1048576
  192.7 21.9 %slice-start = ((s8[4718592]{0:T(1024)(128)(4,1)}), s8[4194304]{0:T(1024)(128)(4,1)S(1)}, s32[]{:S(2)}) async-start(s8[4718592]{0:T(1024)(128)(4,1)} %bitcast.163), calls=%async_computation.7 | async-start | bytes 8388608
  202.4 12.3 %copy-start.2 = (f32[1,32,32,768]{3,2,0,1:T(8,128)S(1)}, f32[1,32,32,768]{3,2,0,1:T(8,128)}, u32[]{:S(2)}) copy-start(f32[1,32,32,768]{3,2,0,1:T(8,128)} %copy.84) | copy-start | bytes 9437188
  202.4 12.3 %slice-start.1 = ((s8[4718592]{0:T(1024)(128)(4,1)}), s8[524288]{0:T(1024)(128)(4,1)S(1)}, s32[]{:S(2)}) async-start(s8[4718592]{0:T(1024)(128)(4,1)} %bitcast.163), calls=%async_computation.8 | async-start | bytes 1048576
  223.6 3.5 copy-start.8
  224.9 1.2 copy-start.4
  227.0 139.0 %all-gather.11.cloned.1.call-start = ((), (), s32[]{:S(2)}) async-start(), calls=%async_computation.4 | async-start | bytes 1474560 | tf_op jit(solution)/shard_map/all_gather | solution.py:207
  238.9 10.1 %copy-start.19 = (bf16[1024,768]{1,0:T(8,128)(2,1)S(1)}, bf16[1024,768]{1,0:T(8,128)(2,1)}, u32[]{:S(2)}) copy-start(bf16[1024,768]{1,0:T(8,128)(2,1)} %get-tuple-element.208) | copy-start | bytes 4718596
  249.0 248.3 %reduce-scatter.4.cloned.1.call-start = ((), (), s32[]{:S(2)}) async-start(), calls=%async_computation.6 | async-start | bytes 19464192
  249.0 7.4 %copy-start.3 = (f32[3072,768]{0,1:T(8,128)S(1)}, f32[3072,768]{0,1:T(8,128)}, u32[]{:S(2)}) copy-start(f32[3072,768]{0,1:T(8,128)} %fusion.64) | copy-start | bytes 28311556
  282.3 0.9 copy-start.12
  282.3 2.9 copy-start.13
  282.3 341.0 %all-reduce.7.cloned.1.call-start = ((), (), s32[]{:S(2)}) async-start(), calls=%async_computation.5 | async-start | bytes 301056 | tf_op jit(solution)/shard_map/psum | solution.py:211
  367.4 24.1 %copy-start.6 = (bf16[1,1,32,32,768]{4,3,2,1,0:T(8,128)(2,1)S(1)}, bf16[1,1,32,32,768]{4,3,2,1,0:T(8,128)(2,1)}, u32[]{:S(2)}) copy-start(bf16[1,1,32,32,768]{4,3,2,1,0:T(8,128)(2,1)} %param.13) | copy-start | bytes 4718596
  367.4 24.1 %copy-start.10 = (f32[7,7,768]{2,1,0:T(8,128)S(1)}, f32[7,7,768]{2,1,0:T(8,128)}, u32[]{:S(2)}) copy-start(f32[7,7,768]{2,1,0:T(8,128)} %rev.3) | copy-start | bytes 451588
  391.5 233.3 %copy-start.1 = (s32[1,4,8]{2,1,0:T(4,128)S(1)}, s32[1,4,8]{2,1,0:T(4,128)}, u32[]{:S(2)}) copy-start(s32[1,4,8]{2,1,0:T(4,128)} %param.14) | copy-start | bytes 388
Sparse Core Ops, SparseCore 0:
  10.4 30.4 all-gather.4
  43.3 27.7 all-gather.6
  227.1 27.7 all-gather.8
  256.6 27.7 all-gather.10
  290.6 206.6 reduce-scatter.3
  503.2 119.9 all-reduce.6
where the time goes:
time: 644 us; the launch traced here: 632 us
  waiting for transfers between devices  220 us (34%)
  matrix products  194 us (30%)
  other arithmetic  89.6 us (14%)
  local copies, waits for them, and re-layouts  57.8 us (9%)
  blocking collectives  40.2 us (6%)
  between operations  30.4 us (5%)
    psum x1, waiting for transfers between devices, on_device(): lax.psum((kernel_sum, channel_sum, up_bias_sum), ('slide', 'tile'))  124 us
    conv_general_dilated x2, matrix products, depthwise(): lax.conv_general_dilated(extended, kernel[:, :, None, :], (1, 1), 'VALID'...  102 us
    unnamed x7, waiting for transfers between devices  73.9 us
    psum x1, blocking collectives, on_device(): lax.psum((kernel_sum, channel_sum, up_bias_sum), ('slide', 'tile'))  40.2 us
    unnamed x66, local copies, waits for them, and re-layouts  34 us
    conv_general_dilated x1, matrix products, kernel_grad(): lax.conv_general_dilated(extended, kernel, (1, 1), 'VALID', dimension_num...  32.8 us
    concatenate x1, other arithmetic, extend(): return jnp.concatenate([upper, middle, lower], 1)  24 us
    conv_general_dilated x1, other arithmetic, depthwise(): lax.conv_general_dilated(extended, kernel[:, :, None, :], (1, 1), 'VALID'...  24 us
  transfers between devices with their start and end apart: 6, of which 3 were waited for; matrix products, arithmetic and copies ran while one was open for 29% of the time, Pallas kernels for 0%

commit v1 on v0

v1 whole, which is shorter than its diff:
```python
import functools

import jax
import jax.numpy as jnp
from jax import lax
from jax.experimental import pallas as pl
from jax.experimental.pallas import tpu as pltpu
from jax.sharding import PartitionSpec as P

ln_eps = 1e-06
root_half = 0.7071067811865476
inv_root_two_pi = 0.3989422804014327
kind_of = (0, 1, 2, 3, 0, 0, 1, 1)
lanes = 128
row_step = 4
vmem_bytes = 56 * 1024 * 1024


def params(**more):
    return pltpu.CompilerParams(vmem_limit_bytes=vmem_bytes, **more)


def exchange_rims(tile, table, me, count):
    side, _, channels = tile.shape
    columns = lambda part: jnp.transpose(part, (1, 0, 2))
    strips = jnp.stack([tile[-3:], tile[:3], columns(tile[:, -3:]), columns(tile[:, :3])])
    strips = strips.reshape(4, 3 * side, channels)
    kinds = jnp.array(kind_of, jnp.int32)
    slots = [jnp.zeros_like(strips[0])]
    for offset in range(1, count):
        peer = lax.rem(me + offset, count)
        rows = lax.dynamic_index_in_dim(table, peer, 0, keepdims=False)
        kind = jnp.sum(jnp.where(rows == me, kinds, 0))
        message = lax.dynamic_index_in_dim(strips, kind, 0, keepdims=False)
        perm = [(i, (i + offset) % count) for i in range(count)]
        slots.append(lax.ppermute(message, "tile", perm))
    slots = jnp.stack(slots).reshape(count, 3, side, channels)
    mine = lax.dynamic_index_in_dim(table, me, 0, keepdims=False)
    place = jnp.where(mine == count, 0, lax.rem(me - mine + count, count))
    strip = [lax.dynamic_index_in_dim(slots, place[d], 0, keepdims=False) for d in range(8)]
    blank = jnp.zeros((3, 5, channels), tile.dtype)

    def edge(left, centre, right):
        whole = jnp.concatenate([blank, left[:, -3:], centre, right[:, :3], blank], 1)
        return whole.astype(jnp.float32)

    top = edge(strip[4], strip[0], strip[5])
    bottom = edge(strip[6], strip[1], strip[7])
    west = jnp.pad(columns(strip[2]), ((0, 0), (5, 0), (0, 0))).astype(jnp.float32)
    east = jnp.pad(columns(strip[3]), ((0, 0), (0, 5), (0, 0))).astype(jnp.float32)
    return top, bottom, west, east


def fill(ext, tile_ref, top_ref, bottom_ref, west_ref, east_ref):
    side = tile_ref.shape[0]
    ext[0:3] = top_ref[...]
    ext[side + 3 : side + 6] = bottom_ref[...]
    ext[3 : side + 3, 0:8] = west_ref[...]
    ext[3 : side + 3, 8 : side + 8] = tile_ref[...].astype(jnp.float32)
    ext[3 : side + 3, side + 8 : side + 16] = east_ref[...]


def conv_body(with_add, tile_ref, top, bottom, west, east, weight_ref, *rest):
    if with_add:
        add_ref, out_ref, ext, shifted, total = rest
    else:
        out_ref, ext, shifted, total = rest
    side = tile_ref.shape[0]
    fill(ext, tile_ref, top, bottom, west, east)
    for b in range(7):
        if b == 3:
            source, base = ext, 8
        else:
            shifted[...] = ext[:, 5 + b : 5 + b + side]
            source, base = shifted, 0
        taps = [
            jnp.broadcast_to(weight_ref[a * 7 + b : a * 7 + b + 1, :], (8, lanes)) for a in range(7)
        ]

        def rows(step, carry, b=b, source=source, base=base, taps=taps):
            first = step * row_step
            for group in range(side // 8):
                at = pl.ds(base + group * 8, 8)
                here = pl.ds(group * 8, 8)
                sums = [None] * row_step
                for r in range(row_step + 6):
                    value = source[first + r, at]
                    for i in range(row_step):
                        a = r - i
                        if 0 <= a < 7:
                            term = value * taps[a]
                            sums[i] = term if sums[i] is None else sums[i] + term
                for i in range(row_step):
                    if b > 0:
                        sums[i] = sums[i] + total[first + i, here]
                    total[first + i, here] = sums[i]
            return carry

        lax.fori_loop(0, side // row_step, rows, 0)
    if with_add:
        out_ref[...] = (add_ref[...].astype(jnp.float32) + total[...]).astype(jnp.bfloat16)
    else:
        out_ref[...] = total[...]


def tile_spec(shape):
    return pl.BlockSpec(shape[:-1] + (lanes,), lambda c: (0,) * (len(shape) - 1) + (c,))


def depthwise(tile, rims, weight, add=None):
    side, _, channels = tile.shape
    operands = [tile, *rims, weight] + ([] if add is None else [add])
    out = jax.ShapeDtypeStruct(tile.shape, jnp.float32 if add is None else jnp.bfloat16)
    flops = 2 * 49 * side * side * channels
    return pl.pallas_call(
        functools.partial(conv_body, add is not None),
        out_shape=out,
        grid=(channels // lanes,),
        in_specs=[tile_spec(o.shape) for o in operands],
        out_specs=tile_spec(out.shape),
        scratch_shapes=[
            pltpu.VMEM((side + 6, side + 16, lanes), jnp.float32),
            pltpu.VMEM((side + 6, side, lanes), jnp.float32),
            pltpu.VMEM((side, side, lanes), jnp.float32),
        ],
        compiler_params=params(),
        cost_estimate=pl.CostEstimate(flops=100 * flops, bytes_accessed=8 << 20, transcendentals=0),
        name="depthwise",
    )(*operands)


def kernel_grad_body(tile_ref, top, bottom, west, east, grad_ref, out_ref, ext, shifted, grad):
    side = tile_ref.shape[0]
    fill(ext, tile_ref, top, bottom, west, east)
    grad[...] = grad_ref[...].astype(jnp.float32)
    for b in range(7):
        if b == 3:
            source, base = ext, 8
        else:
            shifted[...] = ext[:, 5 + b : 5 + b + side]
            source, base = shifted, 0

        def rows(step, sums, source=source, base=base):
            first = step * row_step
            sums = list(sums)
            for group in range(side // 8):
                at = pl.ds(base + group * 8, 8)
                here = pl.ds(group * 8, 8)
                near = [grad[first + i, here] for i in range(row_step)]
                for r in range(row_step + 6):
                    value = source[first + r, at]
                    for i in range(row_step):
                        a = r - i
                        if 0 <= a < 7:
                            slot = a * 2 + i % 2
                            sums[slot] = sums[slot] + value * near[i]
            return tuple(sums)

        zero = jnp.zeros((8, lanes), jnp.float32)
        sums = lax.fori_loop(0, side // row_step, rows, (zero,) * 14)
        for a in range(7):
            out_ref[a * 7 + b : a * 7 + b + 1, :] = jnp.sum(
                sums[2 * a] + sums[2 * a + 1], axis=0, keepdims=True
            )


def kernel_grad(tile, rims, conv_grad):
    side, _, channels = tile.shape
    operands = [tile, *rims, conv_grad]
    flops = 2 * 49 * side * side * channels
    return pl.pallas_call(
        kernel_grad_body,
        out_shape=jax.ShapeDtypeStruct((49, channels), jnp.float32),
        grid=(channels // lanes,),
        in_specs=[tile_spec(o.shape) for o in operands],
        out_specs=tile_spec((49, channels)),
        scratch_shapes=[
            pltpu.VMEM((side + 6, side + 16, lanes), jnp.float32),
            pltpu.VMEM((side + 6, side, lanes), jnp.float32),
            pltpu.VMEM((side, side, lanes), jnp.float32),
        ],
        compiler_params=params(),
        cost_estimate=pl.CostEstimate(flops=100 * flops, bytes_accessed=8 << 20, transcendentals=0),
        name="kernel_grad",
    )(*operands)


def nt(left, right):
    return lax.dot_general(
        left, right, (((1,), (1,)), ((), ())), preferred_element_type=jnp.float32
    )


def nn(left, right):
    return jnp.dot(left, right, preferred_element_type=jnp.float32)


def mlp_body(
    conv_ref,
    x_ref,
    g_ref,
    keep_ref,
    gain_ref,
    shift_ref,
    up_ref,
    up_bias_ref,
    down_ref,
    down_bias_ref,
    scale_ref,
    block_out_ref,
    conv_grad_ref,
    up_grad_ref,
    down_grad_ref,
    sums_ref,
    bias_ref,
    flat,
    branch_grad,
    inv,
    white,
    branch,
    normed_grad,
):
    step = pl.program_id(0)
    pixels, channels = conv_ref.shape
    part = 128

    @pl.when(step == 0)
    def _():
        keep = keep_ref[0:1, 0:1]

        def body(i, total):
            at = pl.ds(pl.multiple_of(i * part, part), part)
            values = conv_ref[at, :]
            centred = values - jnp.mean(values, axis=-1, keepdims=True)
            inv_std = lax.rsqrt(jnp.mean(centred * centred, axis=-1, keepdims=True) + ln_eps)
            whitened = centred * inv_std
            white[at, :] = whitened
            inv[at, :] = jnp.broadcast_to(inv_std, (part, lanes))
            flat[at, :] = (whitened * gain_ref[...] + shift_ref[...]).astype(jnp.bfloat16)
            own = (keep * scale_ref[...] * g_ref[at, :].astype(jnp.float32)).astype(jnp.bfloat16)
            branch_grad[at, :] = own
            return total + jnp.sum(own.astype(jnp.float32), axis=0, keepdims=True)

        zero = jnp.zeros((1, channels), jnp.float32)
        sums_ref[2:3, :] = lax.fori_loop(0, pixels // part, body, zero)
        branch[...] = jnp.zeros_like(branch)
        normed_grad[...] = jnp.zeros_like(normed_grad)

    up, down = up_ref[...], down_ref[...]
    pre = nt(flat[...], up) + up_bias_ref[...]
    act_grad = nn(branch_grad[...], down)
    cdf = 0.5 * (1.0 + lax.erf(pre * root_half))
    slope = cdf + pre * inv_root_two_pi * jnp.exp(-0.5 * pre * pre)
    act = (pre * cdf).astype(jnp.bfloat16)
    pre_grad_wide = act_grad * slope
    pre_grad = pre_grad_wide.astype(jnp.bfloat16)
    branch[...] += nt(act, down)
    normed_grad[...] += nn(pre_grad, up)
    bias_ref[...] = jnp.sum(pre_grad.astype(jnp.float32), axis=0, keepdims=True)
    up_grad_ref[...] = nn(pre_grad.T, flat[...]).astype(jnp.bfloat16)
    down_grad_ref[...] = nn(act.T, branch_grad[...]).astype(jnp.bfloat16)

    @pl.when(step == pl.num_programs(0) - 1)
    def _():
        keep = keep_ref[0:1, 0:1]

        def body(i, totals):
            at = pl.ds(pl.multiple_of(i * part, part), part)
            out = branch[at, :] + down_bias_ref[...]
            g = g_ref[at, :].astype(jnp.float32)
            block_out_ref[at, :] = (
                x_ref[at, :].astype(jnp.float32) + keep * scale_ref[...] * out
            ).astype(jnp.bfloat16)
            whitened = white[at, :]
            own = normed_grad[at, :]
            scaled = own * gain_ref[...]
            spread = whitened * jnp.mean(scaled * whitened, axis=-1, keepdims=True)
            centred = scaled - jnp.mean(scaled, axis=-1, keepdims=True) - spread
            conv_grad_ref[at, :] = (inv[at, 0:1] * centred).astype(jnp.bfloat16)
            down_sum = lambda v: jnp.sum(v, axis=0, keepdims=True)
            terms = (own * whitened, own, g * keep * out)
            return tuple(t + down_sum(v) for t, v in zip(totals, terms))

        zero = jnp.zeros((1, channels), jnp.float32)
        totals = lax.fori_loop(0, pixels // part, body, (zero,) * 3)
        sums_ref[0:1, :] = totals[0]
        sums_ref[1:2, :] = totals[1]
        sums_ref[3:4, :] = totals[2]


def mlp(conv, x, g, keep, gain, shift, up, up_bias, down, down_bias, scale):
    pixels, channels = conv.shape
    hidden = up.shape[0]
    block = 256
    whole = lambda shape: pl.BlockSpec(
        shape, lambda j: (0, 0), pipeline_mode=pl.Buffered(buffer_count=1)
    )
    full = lambda shape: pl.BlockSpec(shape, lambda j: (0, 0))
    row = pl.BlockSpec((1, channels), lambda j: (0, 0))
    return pl.pallas_call(
        mlp_body,
        out_shape=(
            jax.ShapeDtypeStruct((pixels, channels), jnp.bfloat16),
            jax.ShapeDtypeStruct((pixels, channels), jnp.bfloat16),
            jax.ShapeDtypeStruct((hidden, channels), jnp.bfloat16),
            jax.ShapeDtypeStruct((hidden, channels), jnp.bfloat16),
            jax.ShapeDtypeStruct((4, channels), jnp.float32),
            jax.ShapeDtypeStruct((1, hidden), jnp.float32),
        ),
        grid=(hidden // block,),
        in_specs=[
            whole((pixels, channels)),
            whole((pixels, channels)),
            whole((pixels, channels)),
            pl.BlockSpec((1, lanes), lambda j: (0, 0)),
            row,
            row,
            pl.BlockSpec((block, channels), lambda j: (j, 0)),
            pl.BlockSpec((1, block), lambda j: (0, j)),
            pl.BlockSpec((channels, block), lambda j: (0, j)),
            row,
            row,
        ],
        out_specs=(
            full((pixels, channels)),
            full((pixels, channels)),
            pl.BlockSpec((block, channels), lambda j: (j, 0)),
            pl.BlockSpec((block, channels), lambda j: (j, 0)),
            pl.BlockSpec((4, channels), lambda j: (0, 0)),
            pl.BlockSpec((1, block), lambda j: (0, j)),
        ),
        scratch_shapes=[
            pltpu.VMEM((pixels, channels), jnp.bfloat16),
            pltpu.VMEM((pixels, channels), jnp.bfloat16),
            pltpu.VMEM((pixels, lanes), jnp.float32),
            pltpu.VMEM((pixels, channels), jnp.float32),
            pltpu.VMEM((pixels, channels), jnp.float32),
            pltpu.VMEM((pixels, channels), jnp.float32),
        ],
        compiler_params=params(),
        cost_estimate=pl.CostEstimate(
            flops=12 * pixels * channels * hidden,
            bytes_accessed=32 << 20,
            transcendentals=2 * pixels * hidden,
        ),
        name="mlp",
    )(conv, x, g, keep, gain, shift, up, up_bias, down, down_bias, scale)


class Grid:
    def __init__(self, slides, tiles):
        self.sizes = {"rest": slides // 2, "core": 2, "hi": 2, "lo": tiles // 2}
        self.names = ("rest", "core", "hi", "lo")
        slide, tile = lax.axis_index("slide"), lax.axis_index("tile")
        self.place = {
            "rest": slide // 2,
            "core": lax.rem(slide, 2),
            "hi": tile // (tiles // 2),
            "lo": lax.rem(tile, tiles // 2),
        }

    def perm(self, axis, move):
        pairs = []
        extents = [self.sizes[n] for n in self.names]
        at = self.names.index(axis)
        stride = 1
        for size in extents[at + 1 :]:
            stride *= size
        total = 1
        for size in extents:
            total *= size
        for device in range(total):
            own = (device // stride) % extents[at]
            pairs.append((device, device + (move(own) - own) * stride))
        return pairs

    def send(self, value, axis, move):
        return lax.ppermute(value, ("slide", "tile"), self.perm(axis, move))

    def scatter(self, value, dim, axis, last=False):
        size, own = self.sizes[axis], self.place[axis]
        pick = lambda i: lax.dynamic_index_in_dim(value, i, dim, keepdims=False)
        total = pick(own).astype(jnp.float32)
        for offset in range(1, size):
            block = pick(lax.rem(own + offset, size))
            came = self.send(block, axis, lambda i, o=offset: (i + o) % size)
            total = total + came.astype(jnp.float32)
        return total if last else total.astype(jnp.bfloat16)

    def everywhere(self, value):
        for axis in self.names[::-1]:
            step = 1
            while step < self.sizes[axis]:
                value = value + self.send(value, axis, lambda i, s=step: i ^ s)
                step *= 2
        return value


def on_device(
    features,
    cotangent,
    neighbours,
    skip_flags,
    dw_weight,
    ln_gain,
    ln_bias,
    up_weight,
    up_bias,
    down_weight,
    down_bias,
    layer_scale,
):
    slides, tiles = lax.axis_size("slide"), lax.axis_size("tile")
    side, channels = features.shape[3], features.shape[4]
    hidden = up_weight.shape[1]
    me = lax.axis_index("tile")
    table = neighbours[0]
    grid = Grid(slides, tiles)
    tile, grad = features[0, 0], cotangent[0, 0]
    taps = dw_weight[0].reshape(49, channels)
    keep = jnp.broadcast_to((1 - skip_flags[0, 0]).astype(jnp.float32), (1, lanes))

    rims = exchange_rims(tile, table, me, tiles)
    conv = depthwise(tile, rims, taps)
    block_out, conv_grad, up_grad, down_grad, sums, bias = mlp(
        conv.reshape(-1, channels),
        tile.reshape(-1, channels),
        grad.reshape(-1, channels),
        keep,
        ln_gain,
        ln_bias,
        up_weight[0],
        up_bias,
        down_weight[0],
        down_bias,
        layer_scale,
    )
    conv_tile = conv_grad.reshape(side, side, channels)
    grad_rims = exchange_rims(conv_tile, table, me, tiles)

    shape = tuple(grid.sizes[n] for n in grid.names)
    up_part = grid.scatter(up_grad.reshape(*shape, -1, channels), 1, "core")
    down_part = grid.scatter(down_grad.reshape(*shape, -1, channels), 1, "core")
    up_part = grid.scatter(up_part, 1, "hi")
    down_part = grid.scatter(down_part, 2, "lo")
    up_part = grid.scatter(up_part, 1, "lo")
    down_part = grid.scatter(down_part, 1, "hi")
    up_part = grid.scatter(up_part, 0, "rest", last=True)
    down_part = grid.scatter(down_part, 0, "rest", last=True)
    weight_grads = jnp.concatenate([up_part, down_part], -1)[None]

    kernel_sum = kernel_grad(tile, rims, conv_tile)
    small = jnp.concatenate([kernel_sum, sums, bias.reshape(-1, channels)], 0)
    small = grid.everywhere(small)
    input_grad = depthwise(conv_tile, grad_rims, taps[::-1], grad)
    return (
        block_out.reshape(1, 1, side, side, channels),
        input_grad[None, None],
        weight_grads,
        small[:49].reshape(1, 7, 7, channels),
        small[49:53][None],
        small[53:].reshape(1, hidden),
    )


def solution(mesh):
    tiles = P("slide", "tile", None, None, None)
    return jax.shard_map(
        on_device,
        mesh=mesh,
        in_specs=(tiles, tiles, P("slide", None, None), P(None, "slide")) + (P(),) * 8,
        out_specs=(tiles, tiles, P(None, ("slide", "tile"), None), P(), P(), P()),
        check_vma=False,
    )
```

time: 644 us -> 230 us (0.36); the launches traced: 632 us -> 230 us
  matrix products: 194 us -> 0 us
  waiting for transfers between devices: 220 us -> 37.9 us
  Pallas kernels: 0 us -> 97.3 us
  other arithmetic: 89.6 us -> 21.1 us
  blocking collectives: 40.2 us -> 0 us
  local copies, waits for them, and re-layouts: 57.8 us -> 22.9 us
  starting transfers between devices: 0.25 us -> 27.2 us
  between operations: 30.4 us -> 23.1 us
    conv_general_dilated x3 -> x0, matrix products: 135 us -> none  [the longest x2 102 us: depthwise(): lax.conv_general_dilated(extended, kernel[:, :, None, :], (1, 1), 'VALID'...]
    psum x1 -> x0, waiting for transfers between devices: 124 us -> none  [on_device(): lax.psum((kernel_sum, channel_sum, up_bias_sum), ('slide', 'tile'))]
    pallas_call x0 -> x4, Pallas kernels: none -> 97.3 us  [the longest x1 47.5 us: mlp(): pl.pallas_call(mlp_body, out_shape=(jax.ShapeDtypeStruct((pixels, channel...]
    unnamed x7 -> x0, waiting for transfers between devices: 73.9 us -> none
    dot_general x6 -> x0, matrix products: 59 us -> none  [the longest x2 20.4 us: contract(): lax.dot_general(left, right, (((1,), (1,)), ((), ())), preferred_element_...]
    psum x1 -> x0, blocking collectives: 40.2 us -> none  [on_device(): lax.psum((kernel_sum, channel_sum, up_bias_sum), ('slide', 'tile'))]
    ppermute x0 -> x23, waiting for transfers between devices: none -> 37.9 us  [the longest x17 34.2 us: send(): return lax.ppermute(value, ('slide', 'tile'), self.perm(axis, move))]
    unnamed x66 -> x26, local copies, waits for them, and re-layouts: 34 us -> 1.86 us
  transfers between devices with their start and end apart: 6 -> 23, of which waited for: 3 -> 9; matrix products, arithmetic and copies ran while one was open for 29% -> 12% of each run, Pallas kernels for 0% -> 14%
where the time goes in v1:
time: 230 us
  Pallas kernels  97.3 us (42%)
  waiting for transfers between devices  37.9 us (16%)
  starting transfers between devices  27.2 us (12%)
  between operations  23.1 us (10%)
  local copies, waits for them, and re-layouts  22.9 us (10%)
  other arithmetic  21.1 us (9%)
    pallas_call x1, Pallas kernels, mlp(): pl.pallas_call(mlp_body, out_shape=(jax.ShapeDtypeStruct((pixels, channel...  47.5 us
    ppermute x17, waiting for transfers between devices, send(): return lax.ppermute(value, ('slide', 'tile'), self.perm(axis, move))  34.2 us
    pallas_call x2, Pallas kernels, depthwise(): pl.pallas_call(functools.partial(conv_body, add is not None), out_shape=o...  33.6 us
    ppermute x17, starting transfers between devices, send(): return lax.ppermute(value, ('slide', 'tile'), self.perm(axis, move))  19.1 us
    pallas_call x1, Pallas kernels, kernel_grad(): pl.pallas_call(kernel_grad_body, out_shape=jax.ShapeDtypeStruct((49, chan...  16.3 us
    convert_element_type x6, other arithmetic, scatter(): return total if last else total.astype(jnp.bfloat16)  8.34 us
    ppermute x6, starting transfers between devices, exchange_rims(): slots.append(lax.ppermute(message, 'tile', perm))  8.06 us
    dynamic_slice x4, local copies, waits for them, and re-layouts, scatter(): pick = lambda i: lax.dynamic_index_in_dim(value, i, dim, keepdims=False)  7.85 us
  transfers between devices with their start and end apart: 23, of which 9 were waited for; matrix products, arithmetic and copies ran while one was open for 12% of the time, Pallas kernels for 14%

profile of v1, /device:TPU:0, one launch (start us, length us, event | category | flops | bytes accessed | tf_op | source)
XLA Modules:
  0.0 229.5 jit_solution(7739491465783930650)
XLA Ops:
  0.7 1.5 fusion.10
  6.0 1.0 fusion.15
  7.0 1.3 slice_bitcast_fusion.3
  10.4 3.0 %collective-permute-start.1 = (bf16[96,768]{1,0:T(8,128)(2,1)S(1)}, bf16[96,768]{1,0:T(8,128)(2,1)S(1)}, u32[]{:S(2)}, u32[]{:S(2)}) collective-permute-start(bf16[96,768]{1,0:T(8,128)(2,1)S(1)} %get-tuple-element.72), channel_id=1, source_target_pairs={{0,2},{1,3},{2,0},{3,1},{4,6},{5,7},{6,4},{7,5},{8,10},{9,11},{10,... | collective-permute-start | bytes 442376 | tf_op jit(solution)/shard_map/ppermute | solution.py:36
  13.5 1.4 collective-permute-start.2
  14.9 0.6 collective-permute-start
  15.5 0.7 bitcast_select_fusion
  16.2 0.6 fusion.16
  28.2 2.0 rev.3.weight_ref
  35.8 0.9 pad_convert_fusion.2.east
  36.8 1.0 pad_convert_fusion.3.west
  38.0 0.8 convert_element_type.139.bottom
  39.0 0.8 convert_element_type.138.top
  39.8 16.7 %depthwise.2 = f32[32,32,768]{2,1,0:T(8,128)} custom-call(bf16[32,32,768]{2,1,0:T(8,128)(2,1)} %bitcast.179, f32[3,48,768]{2,1,0:T(8,128)} %convert_element_type.138.top, f32[3,48,768]{2,1,0:T(8,128)} %convert_element_type.139.bottom, f32[32,8,768]{2,1,0:T(8,128)} %pad_convert_fusion.3.west, f32[32,8,768]{2,1,0:T(8,128)} %pad_convert_fusion.2.east, ...), custom_call_target="tpu_custom_call" | custom-call | flops 7707033600 | bytes 8388608 | tf_op jit(solution)/shard_map/depthwise/pallas_call | solution.py:115
  56.5 0.5 broadcast_in_dim.25.keep_ref
  57.0 47.5 %mlp.1 = (bf16[1024,768]{1,0:T(8,128)(2,1)}, bf16[1024,768]{1,0:T(8,128)(2,1)}, bf16[3072,768]{1,0:T(8,128)(2,1)}, bf16[3072,768]{1,0:T(8,128)(2,1)}, f32[4,768]{1,0:T(4,128)}, /*index=5*/f32[1,3072]{1,0:T(1,128)}) custom-call(f32[1024,768]{1,0:T(8,128)} %bitcast.196, bf16[1024,768]{1,0:T(8,128)(2,1)} %bitcast.180, bf16[1024,768]{1,0:T(8,128)(2,1)} %bitcast.194, ...), custom_call_target="tpu_custom_call" | custom-call | flops 28991029248 | bytes 33554432 | tf_op jit(solution)/shard_map/mlp/pallas_call | solution.py:300
  104.5 4.2 %constant_dynamic-slice_fusion.3 = (bf16[4,1,2,2,96,768]{5,4,3,2,1,0:T(8,128)(2,1)}, bf16[4,1,2,2,96,768]{5,4,3,2,1,0:T(8,128)(2,1)S(1)}) fusion(bf16[4,2,2,2,96,768]{5,4,3,2,1,0:T(8,128)(2,1)} %bitcast.169, s32[]{:T(128)S(6)} %select_n.170, s32[]{:T(128)S(6)} %select_n.171), kind=kLoop, calls=%fused_computation.75 | loop fusion | bytes 9437192 | tf_op jit(solution)/shard_map/jit(dynamic_index_in_dim)/dynamic_slice | solution.py:382
  108.7 1.6 copy.67
  110.8 1.6 copy.66
  112.4 0.5 collective-permute-start.12
  112.8 16.3 %kernel_grad.1 = f32[49,768]{1,0:T(8,128)} custom-call(bf16[32,32,768]{2,1,0:T(8,128)(2,1)} %bitcast.181, f32[3,48,768]{2,1,0:T(8,128)} %convert_element_type.138.top, f32[3,48,768]{2,1,0:T(8,128)} %convert_element_type.139.bottom, f32[32,8,768]{2,1,0:T(8,128)} %pad_convert_fusion.3.west, f32[32,8,768]{2,1,0:T(8,128)} %pad_convert_fusion.2.east, ...), custom_call_target="tpu_custom_call" | custom-call | flops 7707033600 | bytes 8388608 | tf_op jit(solution)/shard_map/kernel_grad/pallas_call | solution.py:171
  129.1 0.5 broadcast.56
  129.6 0.7 reduce.7
  130.3 0.9 pad_maximum_fusion.4
  131.3 2.5 %collective-permute-start.18 = (f32[57,768]{1,0:T(8,128)S(1)}, f32[57,768]{1,0:T(8,128)S(1)}, u32[]{:S(2)}, u32[]{:S(2)}) collective-permute-start(f32[57,768]{1,0:T(8,128)S(1)} %pad_maximum_fusion.4), channel_id=1, source_target_pairs={{0,1},{1,0},{2,3},{3,2},{4,5},{5,4},{6,7},{7,6},{8,9},{9,8},{10,11... | collective-permute-start | bytes 525320 | tf_op jit(solution)/shard_map/ppermute | solution.py:378
  133.7 1.3 slice_bitcast_fusion.1
  135.1 1.0 slice_bitcast_fusion.5
  136.3 0.6 collective-permute-start.4
  136.8 2.2 collective-permute-done.18
  139.1 2.4 %collective-permute-start.5 = (bf16[96,768]{1,0:T(8,128)(2,1)S(1)}, bf16[96,768]{1,0:T(8,128)(2,1)S(1)}, u32[]{:S(2)}, u32[]{:S(2)}) collective-permute-start(bf16[96,768]{1,0:T(8,128)(2,1)S(1)} %get-tuple-element.60), channel_id=1, source_target_pairs={{0,3},{1,0},{2,1},{3,2},{4,7},{5,4},{6,5},{7,6},{8,11},{9,8},{10,9... | collective-permute-start | bytes 442376 | tf_op jit(solution)/shard_map/ppermute | solution.py:36
  141.5 2.4 %collective-permute-done.3 = bf16[96,768]{1,0:T(8,128)(2,1)S(1)} collective-permute-done((bf16[96,768]{1,0:T(8,128)(2,1)S(1)}, bf16[96,768]{1,0:T(8,128)(2,1)S(1)}, u32[]{:S(2)}, u32[]{:S(2)}) %collective-permute-start.3) | collective-permute-done | bytes 147488 | tf_op jit(solution)/shard_map/ppermute | solution.py:36
  143.9 0.5 collective-permute-start.19
  144.5 1.3 collective-permute-done.4
  145.9 3.7 %collective-permute-done.19 = f32[57,768]{1,0:T(8,128)S(1)} collective-permute-done((f32[57,768]{1,0:T(8,128)S(1)}, f32[57,768]{1,0:T(8,128)S(1)}, u32[]{:S(2)}, u32[]{:S(2)}) %collective-permute-start.19) | collective-permute-done | bytes 175136 | tf_op jit(solution)/shard_map/ppermute | solution.py:378
  150.1 0.9 pad_convert_fusion.east
  151.1 1.7 collective-permute-start.21
  152.8 2.4 %fusion.1 = bf16[4,2,2,96,768]{4,3,0,2,1:T(8,128)(2,1)S(1)} fusion(bf16[4,2,2,96,768]{4,3,0,2,1:T(8,128)(2,1)} %collective-permute-done.6, bf16[4,1,2,2,96,768]{5,4,3,2,1,0:T(8,128)(2,1)S(1)} %copy-done), kind=kLoop, calls=%fused_computation.3 | loop fusion | flops 4718592 | bytes 7077888 | tf_op jit(solution)/shard_map/convert_element_type | solution.py:388
  155.2 1.3 dynamic-slice_bitcast_fusion.1
  156.5 0.5 collective-permute-start.7
  157.0 2.4 %fusion = bf16[4,2,2,96,768]{4,3,0,1,2:T(8,128)(2,1)S(1)} fusion(bf16[4,2,2,96,768]{4,3,0,1,2:T(8,128)(2,1)} %collective-permute-done.12, bf16[4,1,2,2,96,768]{5,4,3,2,1,0:T(8,128)(2,1)S(1)} %get-tuple-element.35), kind=kLoop, calls=%fused_computation.1 | loop fusion | flops 4718592 | bytes 7077888 | tf_op jit(solution)/shard_map/convert_element_type | solution.py:388
  159.4 1.2 dynamic-slice_bitcast_fusion
  160.6 0.6 copy-done.3
  161.2 2.4 %collective-permute-start.13 = (bf16[4,2,96,768]{3,2,0,1:T(8,128)(2,1)}, bf16[4,2,96,768]{3,2,0,1:T(8,128)(2,1)}, u32[]{:S(2)}, u32[]{:S(2)}) collective-permute-start(bf16[4,2,96,768]{3,2,0,1:T(8,128)(2,1)} %dynamic-slice_bitcast_fusion), channel_id=1, source_target_pairs={{0,1},{1,0},{2,3},{3,2},{4,5},{5,4},{6,7},{7,6},{8,9},{9,8},{10,11... | collective-permute-start | bytes 3538952 | tf_op jit(solution)/shard_map/ppermute | solution.py:378
  163.6 1.0 pad_convert_fusion.1.west
  164.8 0.8 convert_element_type.145.bottom
  165.8 0.8 convert_element_type.144.top
  166.6 2.7 %collective-permute-start.22 = (f32[57,768]{1,0:T(8,128)S(1)}, f32[57,768]{1,0:T(8,128)S(1)}, u32[]{:S(2)}, u32[]{:S(2)}) collective-permute-start(f32[57,768]{1,0:T(8,128)S(1)} %add.271), channel_id=1, source_target_pairs={{0,16},{1,17},{2,18},{3,19},{4,20},{5,21},{6,22},{7,23},{8,24},{9,... | collective-permute-start | bytes 525320 | tf_op jit(solution)/shard_map/ppermute | solution.py:378
  169.2 16.9 %depthwise.3 = bf16[32,32,768]{2,1,0:T(8,128)(2,1)} custom-call(bf16[32,32,768]{2,1,0:T(8,128)(2,1)} %bitcast.184, f32[3,48,768]{2,1,0:T(8,128)} %convert_element_type.144.top, f32[3,48,768]{2,1,0:T(8,128)} %convert_element_type.145.bottom, f32[32,8,768]{2,1,0:T(8,128)} %pad_convert_fusion.1.west, f32[32,8,768]{2,1,0:T(8,128)} %pad_convert_fusion.east, ...), custom_call_target="tpu_custom_call" | custom-call | flops 7707033600 | bytes 8388608 | tf_op jit(solution)/shard_map/depthwise/pallas_call | solution.py:115
  186.1 0.8 reshape.142
  187.0 1.7 fusion.3
  188.8 1.0 collective-permute-done.13
  189.8 1.6 fusion.2
  191.5 0.9 collective-permute-start.14
  192.4 0.6 slice_bitcast_fusion.6
  193.0 0.6 copy.53
  193.6 9.7 %collective-permute-done.8 = bf16[4,96,768]{2,1,0:T(8,128)(2,1)S(1)} collective-permute-done((bf16[4,96,768]{2,1,0:T(8,128)(2,1)S(1)}, bf16[4,96,768]{2,1,0:T(8,128)(2,1)S(1)}, u32[]{:S(2)}, u32[]{:S(2)}) %collective-permute-start.8) | collective-permute-done | bytes 589856 | tf_op jit(solution)/shard_map/ppermute | solution.py:378
  203.5 1.7 collective-permute-start.10
  205.2 1.1 collective-permute-start.11
  206.3 0.9 collective-permute-start.9
  207.4 0.5 collective-permute-start.15
  207.9 3.1 %collective-permute-start.16 = (bf16[96,768]{1,0:T(8,128)(2,1)S(1)}, bf16[96,768]{1,0:T(8,128)(2,1)S(1)}, u32[]{:S(2)}, u32[]{:S(2)}) collective-permute-start(bf16[96,768]{1,0:T(8,128)(2,1)S(1)} %get-tuple-element.50), channel_id=1, source_target_pairs={{0,16},{1,17},{2,18},{3,19},{4,20},{5,21},{6,22},{7,23},{8,24},{9,... | collective-permute-start | bytes 442376 | tf_op jit(solution)/shard_map/ppermute | solution.py:378
  211.0 9.7 %collective-permute-done.10 = bf16[96,768]{1,0:T(8,128)(2,1)S(1)} collective-permute-done((bf16[96,768]{1,0:T(8,128)(2,1)S(1)}, bf16[96,768]{1,0:T(8,128)(2,1)S(1)}, u32[]{:S(2)}, u32[]{:S(2)}) %collective-permute-start.10) | collective-permute-done | bytes 147488 | tf_op jit(solution)/shard_map/ppermute | solution.py:378
  220.8 7.8 %collective-permute-done.16 = bf16[96,768]{1,0:T(8,128)(2,1)S(1)} collective-permute-done((bf16[96,768]{1,0:T(8,128)(2,1)S(1)}, bf16[96,768]{1,0:T(8,128)(2,1)S(1)}, u32[]{:S(2)}, u32[]{:S(2)}) %collective-permute-start.16) | collective-permute-done | bytes 147488 | tf_op jit(solution)/shard_map/ppermute | solution.py:378
  228.7 0.9 maximum_bitcast_fusion
  (91 shorter events, 4.0 us)
Async XLA Ops:
  0.6 26.5 %copy-start.7 = (f32[1,7,7,768]{3,0,2,1:T(1,128)S(1)}, f32[1,7,7,768]{3,0,2,1:T(1,128)}, u32[]{:S(2)}) copy-start(f32[1,7,7,768]{3,0,2,1:T(1,128)} %param.18) | copy-start | bytes 451588
  10.4 24.9 %collective-permute-start.1 = (bf16[96,768]{1,0:T(8,128)(2,1)S(1)}, bf16[96,768]{1,0:T(8,128)(2,1)S(1)}, u32[]{:S(2)}, u32[]{:S(2)}) collective-permute-start(bf16[96,768]{1,0:T(8,128)(2,1)S(1)} %get-tuple-element.72), channel_id=1, source_target_pairs={{0,2},{1,3},{2,0},{3,1},{4,6},{5,7},{6,4},{7,5},{8,10},{9,11},{10,... | collective-permute-start | bytes 442376 | tf_op jit(solution)/shard_map/ppermute | solution.py:36
  13.5 21.9 %collective-permute-start.2 = (bf16[96,768]{1,0:T(8,128)(2,1)S(1)}, bf16[96,768]{1,0:T(8,128)(2,1)S(1)}, u32[]{:S(2)}, u32[]{:S(2)}) collective-permute-start(bf16[96,768]{1,0:T(8,128)(2,1)S(1)} %get-tuple-element.71), channel_id=1, source_target_pairs={{0,3},{1,0},{2,1},{3,2},{4,7},{5,4},{6,5},{7,6},{8,11},{9,8},{10,9... | collective-permute-start | bytes 442376 | tf_op jit(solution)/shard_map/ppermute | solution.py:36
  14.9 20.4 %collective-permute-start = (bf16[96,768]{1,0:T(8,128)(2,1)S(1)}, bf16[96,768]{1,0:T(8,128)(2,1)S(1)}, u32[]{:S(2)}, u32[]{:S(2)}) collective-permute-start(bf16[96,768]{1,0:T(8,128)(2,1)S(1)} %get-tuple-element.70), channel_id=1, source_target_pairs={{0,1},{1,2},{2,3},{3,0},{4,5},{5,6},{6,7},{7,4},{8,9},{9,10},{10,1... | collective-permute-start | bytes 442376 | tf_op jit(solution)/shard_map/ppermute | solution.py:36
  27.5 9.3 %copy-start.5 = (f32[49,768]{1,0:T(8,128)}, f32[49,768]{1,0:T(8,128)S(1)}, u32[]{:S(2)}) copy-start(f32[49,768]{1,0:T(8,128)S(1)} %reshape_squeeze.9.weight_ref) | copy-start | bytes 451588
  104.5 5.9 %slice-start = ((s8[4718592]{0:T(1024)(128)(4,1)}), s8[4194304]{0:T(1024)(128)(4,1)S(1)}, s32[]{:S(2)}) async-start(s8[4718592]{0:T(1024)(128)(4,1)} %bitcast.166), calls=%async_computation | async-start | bytes 8388608
  104.5 5.9 %slice-start.1 = ((s8[4718592]{0:T(1024)(128)(4,1)}), s8[524288]{0:T(1024)(128)(4,1)S(1)}, s32[]{:S(2)}) async-start(s8[4718592]{0:T(1024)(128)(4,1)} %bitcast.166), calls=%async_computation.1 | async-start | bytes 1048576
  110.3 42.5 %collective-permute-start.6 = (bf16[4,2,2,96,768]{4,3,0,2,1:T(8,128)(2,1)}, bf16[4,2,2,96,768]{4,3,0,2,1:T(8,128)(2,1)}, u32[]{:S(2)}, u32[]{:S(2)}) collective-permute-start(bf16[4,2,2,96,768]{4,3,0,2,1:T(8,128)(2,1)} %bitcast.163), channel_id=1, source_target_pairs={{0,4},{1,5},{2,6},{3,7},{4,0},{5,1},{6,2},{7,3},{8,12},{9,13},{10,... | collective-permute-start | bytes 7077896 | tf_op jit(solution)/shard_map/ppermute | solution.py:378
  112.4 44.6 %collective-permute-start.12 = (bf16[4,2,2,96,768]{4,3,0,1,2:T(8,128)(2,1)}, bf16[4,2,2,96,768]{4,3,0,1,2:T(8,128)(2,1)}, u32[]{:S(2)}, u32[]{:S(2)}) collective-permute-start(bf16[4,2,2,96,768]{4,3,0,1,2:T(8,128)(2,1)} %bitcast.162), channel_id=1, source_target_pairs={{0,4},{1,5},{2,6},{3,7},{4,0},{5,1},{6,2},{7,3},{8,12},{9,13},{10,... | collective-permute-start | bytes 7077896 | tf_op jit(solution)/shard_map/ppermute | solution.py:378
  112.8 16.8 %copy-start.9 = (f32[1,3072]{1,0:T(1,128)S(1)}, f32[1,3072]{1,0:T(1,128)}, u32[]{:S(2)}) copy-start(f32[1,3072]{1,0:T(1,128)} %get-tuple-element.17) | copy-start | bytes 36868
  112.8 17.5 %copy-start.8 = (f32[4,768]{1,0:T(4,128)S(1)}, f32[4,768]{1,0:T(4,128)}, u32[]{:S(2)}) copy-start(f32[4,768]{1,0:T(4,128)} %get-tuple-element.16) | copy-start | bytes 36868
  129.1 12.3 %copy-start.6 = (f32[49,768]{1,0:T(8,128)S(1)}, f32[49,768]{1,0:T(8,128)}, u32[]{:S(2)}) copy-start(f32[49,768]{1,0:T(8,128)} %kernel_grad.1) | copy-start | bytes 451588
  131.3 7.8 %collective-permute-start.18 = (f32[57,768]{1,0:T(8,128)S(1)}, f32[57,768]{1,0:T(8,128)S(1)}, u32[]{:S(2)}, u32[]{:S(2)}) collective-permute-start(f32[57,768]{1,0:T(8,128)S(1)} %pad_maximum_fusion.4), channel_id=1, source_target_pairs={{0,1},{1,0},{2,3},{3,2},{4,5},{5,4},{6,7},{7,6},{8,9},{9,8},{10,11... | collective-permute-start | bytes 525320 | tf_op jit(solution)/shard_map/ppermute | solution.py:378
  136.2 7.7 %collective-permute-start.3 = (bf16[96,768]{1,0:T(8,128)(2,1)S(1)}, bf16[96,768]{1,0:T(8,128)(2,1)S(1)}, u32[]{:S(2)}, u32[]{:S(2)}) collective-permute-start(bf16[96,768]{1,0:T(8,128)(2,1)S(1)} %get-tuple-element.59), channel_id=1, source_target_pairs={{0,1},{1,2},{2,3},{3,0},{4,5},{5,6},{6,7},{7,4},{8,9},{9,10},{10,1... | collective-permute-start | bytes 442376 | tf_op jit(solution)/shard_map/ppermute | solution.py:36
  136.3 9.4 %collective-permute-start.4 = (bf16[96,768]{1,0:T(8,128)(2,1)S(1)}, bf16[96,768]{1,0:T(8,128)(2,1)S(1)}, u32[]{:S(2)}, u32[]{:S(2)}) collective-permute-start(bf16[96,768]{1,0:T(8,128)(2,1)S(1)} %get-tuple-element.61), channel_id=1, source_target_pairs={{0,2},{1,3},{2,0},{3,1},{4,6},{5,7},{6,4},{7,5},{8,10},{9,11},{10,... | collective-permute-start | bytes 442376 | tf_op jit(solution)/shard_map/ppermute | solution.py:36
  139.1 6.7 %collective-permute-start.5 = (bf16[96,768]{1,0:T(8,128)(2,1)S(1)}, bf16[96,768]{1,0:T(8,128)(2,1)S(1)}, u32[]{:S(2)}, u32[]{:S(2)}) collective-permute-start(bf16[96,768]{1,0:T(8,128)(2,1)S(1)} %get-tuple-element.60), channel_id=1, source_target_pairs={{0,3},{1,0},{2,1},{3,2},{4,7},{5,4},{6,5},{7,6},{8,11},{9,8},{10,9... | collective-permute-start | bytes 442376 | tf_op jit(solution)/shard_map/ppermute | solution.py:36
  143.9 5.7 %collective-permute-start.19 = (f32[57,768]{1,0:T(8,128)S(1)}, f32[57,768]{1,0:T(8,128)S(1)}, u32[]{:S(2)}, u32[]{:S(2)}) collective-permute-start(f32[57,768]{1,0:T(8,128)S(1)} %fusion.14), channel_id=1, source_target_pairs={{0,2},{1,3},{2,0},{3,1},{4,6},{5,7},{6,4},{7,5},{8,10},{9,11},{10,... | collective-permute-start | bytes 525320 | tf_op jit(solution)/shard_map/ppermute | solution.py:378
  149.6 3.2 %copy-start = (bf16[4,1,2,2,96,768]{5,4,3,2,1,0:T(8,128)(2,1)S(1)}, bf16[4,1,2,2,96,768]{5,4,3,2,1,0:T(8,128)(2,1)}, u32[]{:S(2)}) copy-start(bf16[4,1,2,2,96,768]{5,4,3,2,1,0:T(8,128)(2,1)} %get-tuple-element.33) | copy-start | bytes 7077892
  149.6 1.5 collective-permute-start.20
  151.1 15.4 %collective-permute-start.21 = (f32[57,768]{1,0:T(8,128)S(1)}, f32[57,768]{1,0:T(8,128)S(1)}, u32[]{:S(2)}, u32[]{:S(2)}) collective-permute-start(f32[57,768]{1,0:T(8,128)S(1)} %add.270), channel_id=1, source_target_pairs={{0,8},{1,9},{2,10},{3,11},{4,12},{5,13},{6,14},{7,15},{8,0},{9,1},... | collective-permute-start | bytes 525320 | tf_op jit(solution)/shard_map/ppermute | solution.py:378
  155.2 4.2 %copy-start.1 = (bf16[4,2,2,96,768]{4,3,0,2,1:T(8,128)(2,1)}, bf16[4,2,2,96,768]{4,3,0,2,1:T(8,128)(2,1)S(1)}, u32[]{:S(2)}) copy-start(bf16[4,2,2,96,768]{4,3,0,2,1:T(8,128)(2,1)S(1)} %fusion.1) | copy-start | bytes 7077892
  156.5 30.5 %collective-permute-start.7 = (bf16[4,2,96,768]{3,2,0,1:T(8,128)(2,1)}, bf16[4,2,96,768]{3,2,0,1:T(8,128)(2,1)}, u32[]{:S(2)}, u32[]{:S(2)}) collective-permute-start(bf16[4,2,96,768]{3,2,0,1:T(8,128)(2,1)} %dynamic-slice_bitcast_fusion.1), channel_id=1, source_target_pairs={{0,2},{1,3},{2,0},{3,1},{4,6},{5,7},{6,4},{7,5},{8,10},{9,11},{10,... | collective-permute-start | bytes 3538952 | tf_op jit(solution)/shard_map/ppermute | solution.py:378
  159.4 1.8 copy-start.3
  161.2 28.6 %collective-permute-start.13 = (bf16[4,2,96,768]{3,2,0,1:T(8,128)(2,1)}, bf16[4,2,96,768]{3,2,0,1:T(8,128)(2,1)}, u32[]{:S(2)}, u32[]{:S(2)}) collective-permute-start(bf16[4,2,96,768]{3,2,0,1:T(8,128)(2,1)} %dynamic-slice_bitcast_fusion), channel_id=1, source_target_pairs={{0,1},{1,0},{2,3},{3,2},{4,5},{5,4},{6,7},{7,6},{8,9},{9,8},{10,11... | collective-permute-start | bytes 3538952 | tf_op jit(solution)/shard_map/ppermute | solution.py:378
  166.6 19.5 %collective-permute-start.22 = (f32[57,768]{1,0:T(8,128)S(1)}, f32[57,768]{1,0:T(8,128)S(1)}, u32[]{:S(2)}, u32[]{:S(2)}) collective-permute-start(f32[57,768]{1,0:T(8,128)S(1)} %add.271), channel_id=1, source_target_pairs={{0,16},{1,17},{2,18},{3,19},{4,20},{5,21},{6,22},{7,23},{8,24},{9,... | collective-permute-start | bytes 525320 | tf_op jit(solution)/shard_map/ppermute | solution.py:378
  169.2 17.7 %copy-start.2 = (bf16[4,2,2,96,768]{4,3,0,2,1:T(8,128)(2,1)S(1)}, bf16[4,2,2,96,768]{4,3,0,2,1:T(8,128)(2,1)}, u32[]{:S(2)}) copy-start(bf16[4,2,2,96,768]{4,3,0,2,1:T(8,128)(2,1)} %copy-done.1) | copy-start | bytes 7077892
  187.0 2.8 %copy-start.4 = (bf16[4,2,2,96,768]{4,3,0,1,2:T(8,128)(2,1)S(1)}, bf16[4,2,2,96,768]{4,3,0,1,2:T(8,128)(2,1)}, u32[]{:S(2)}) copy-start(bf16[4,2,2,96,768]{4,3,0,1,2:T(8,128)(2,1)} %copy-done.3) | copy-start | bytes 7077892
  188.7 14.5 %collective-permute-start.8 = (bf16[4,96,768]{2,1,0:T(8,128)(2,1)S(1)}, bf16[4,96,768]{2,1,0:T(8,128)(2,1)S(1)}, u32[]{:S(2)}, u32[]{:S(2)}) collective-permute-start(bf16[4,96,768]{2,1,0:T(8,128)(2,1)S(1)} %dynamic-slice_bitcast_fusion.3), channel_id=1, source_target_pairs={{0,1},{1,0},{2,3},{3,2},{4,5},{5,4},{6,7},{7,6},{8,9},{9,8},{10,11... | collective-permute-start | bytes 1769480 | tf_op jit(solution)/shard_map/ppermute | solution.py:378
  191.5 15.8 %collective-permute-start.14 = (bf16[4,96,768]{2,1,0:T(8,128)(2,1)S(1)}, bf16[4,96,768]{2,1,0:T(8,128)(2,1)S(1)}, u32[]{:S(2)}, u32[]{:S(2)}) collective-permute-start(bf16[4,96,768]{2,1,0:T(8,128)(2,1)S(1)} %dynamic-slice_bitcast_fusion.2), channel_id=1, source_target_pairs={{0,2},{1,3},{2,0},{3,1},{4,6},{5,7},{6,4},{7,5},{8,10},{9,11},{10,... | collective-permute-start | bytes 1769480 | tf_op jit(solution)/shard_map/ppermute | solution.py:378
  203.5 17.2 %collective-permute-start.10 = (bf16[96,768]{1,0:T(8,128)(2,1)S(1)}, bf16[96,768]{1,0:T(8,128)(2,1)S(1)}, u32[]{:S(2)}, u32[]{:S(2)}) collective-permute-start(bf16[96,768]{1,0:T(8,128)(2,1)S(1)} %get-tuple-element.47), channel_id=1, source_target_pairs={{0,16},{1,17},{2,18},{3,19},{4,20},{5,21},{6,22},{7,23},{8,24},{9,... | collective-permute-start | bytes 442376 | tf_op jit(solution)/shard_map/ppermute | solution.py:378
  205.2 15.5 %collective-permute-start.11 = (bf16[96,768]{1,0:T(8,128)(2,1)S(1)}, bf16[96,768]{1,0:T(8,128)(2,1)S(1)}, u32[]{:S(2)}, u32[]{:S(2)}) collective-permute-start(bf16[96,768]{1,0:T(8,128)(2,1)S(1)} %get-tuple-element.46), channel_id=1, source_target_pairs={{0,24},{1,25},{2,26},{3,27},{4,28},{5,29},{6,30},{7,31},{8,0},{9,1... | collective-permute-start | bytes 442376 | tf_op jit(solution)/shard_map/ppermute | solution.py:378
  206.3 14.4 %collective-permute-start.9 = (bf16[96,768]{1,0:T(8,128)(2,1)S(1)}, bf16[96,768]{1,0:T(8,128)(2,1)S(1)}, u32[]{:S(2)}, u32[]{:S(2)}) collective-permute-start(bf16[96,768]{1,0:T(8,128)(2,1)S(1)} %get-tuple-element.45), channel_id=1, source_target_pairs={{0,8},{1,9},{2,10},{3,11},{4,12},{5,13},{6,14},{7,15},{8,16},{9,17... | collective-permute-start | bytes 442376 | tf_op jit(solution)/shard_map/ppermute | solution.py:378
  207.4 13.4 %collective-permute-start.15 = (bf16[96,768]{1,0:T(8,128)(2,1)S(1)}, bf16[96,768]{1,0:T(8,128)(2,1)S(1)}, u32[]{:S(2)}, u32[]{:S(2)}) collective-permute-start(bf16[96,768]{1,0:T(8,128)(2,1)S(1)} %get-tuple-element.48), channel_id=1, source_target_pairs={{0,8},{1,9},{2,10},{3,11},{4,12},{5,13},{6,14},{7,15},{8,16},{9,17... | collective-permute-start | bytes 442376 | tf_op jit(solution)/shard_map/ppermute | solution.py:378
  207.9 20.6 %collective-permute-start.16 = (bf16[96,768]{1,0:T(8,128)(2,1)S(1)}, bf16[96,768]{1,0:T(8,128)(2,1)S(1)}, u32[]{:S(2)}, u32[]{:S(2)}) collective-permute-start(bf16[96,768]{1,0:T(8,128)(2,1)S(1)} %get-tuple-element.50), channel_id=1, source_target_pairs={{0,16},{1,17},{2,18},{3,19},{4,20},{5,21},{6,22},{7,23},{8,24},{9,... | collective-permute-start | bytes 442376 | tf_op jit(solution)/shard_map/ppermute | solution.py:378
  220.7 7.9 %collective-permute-start.17 = (bf16[96,768]{1,0:T(8,128)(2,1)S(1)}, bf16[96,768]{1,0:T(8,128)(2,1)S(1)}, u32[]{:S(2)}, u32[]{:S(2)}) collective-permute-start(bf16[96,768]{1,0:T(8,128)(2,1)S(1)} %get-tuple-element.49), channel_id=1, source_target_pairs={{0,24},{1,25},{2,26},{3,27},{4,28},{5,29},{6,30},{7,31},{8,0},{9,1... | collective-permute-start | bytes 442376 | tf_op jit(solution)/shard_map/ppermute | solution.py:378

commit v2 on v1

--- a/solution.py
+++ b/solution.py
@@ -13,42 +13,100 @@
 kind_of = (0, 1, 2, 3, 0, 0, 1, 1)
 lanes = 128
 row_step = 4
-vmem_bytes = 56 * 1024 * 1024
+vmem_bytes = 60 * 1024 * 1024
 
 
 def params(**more):
     return pltpu.CompilerParams(vmem_limit_bytes=vmem_bytes, **more)
 
 
-def exchange_rims(tile, table, me, count):
+def rim_body(
+    count, table, tile, top, bottom, west, east, strips, sends, slots, send_sem, recv_sem
+):
+    side = tile.shape[0]
+    me = lax.axis_index("tile")
+    peers = [lax.rem(me + offset, count) for offset in range(1, count)]
+    barrier = pltpu.get_barrier_semaphore()
+    for peer in peers:
+        pl.semaphore_signal(
+            barrier, inc=1, device_id={"tile": peer}, device_id_type=pl.DeviceIdType.MESH
+        )
+    for k in range(3):
+        at = pl.ds(k * side, side)
+        strips[0, at] = tile[side - 3 + k].astype(jnp.float32)
+        strips[1, at] = tile[k].astype(jnp.float32)
+    for h in range(side):
+        row = tile[h].astype(jnp.float32)
+        strips[2, 3 * h : 3 * h + 3] = row[side - 3 :]
+        strips[3, 3 * h : 3 * h + 3] = row[:3]
+    slots[0] = jnp.zeros(slots.shape[1:], slots.dtype)
+    pl.semaphore_wait(barrier, count - 1)
+    copies = []
+    for i, peer in enumerate(peers):
+        kind = jnp.int32(0)
+        for d in range(8):
+            kind = jnp.where(table[peer, d] == me, kind_of[d], kind)
+        sends[i] = strips[kind].astype(jnp.bfloat16)
+        copy = pltpu.make_async_remote_copy(
+            src_ref=sends.at[i],
+            dst_ref=slots.at[i + 1],
+            send_sem=send_sem.at[i],
+            recv_sem=recv_sem.at[i],
+            device_id={"tile": peer},
+            device_id_type=pl.DeviceIdType.MESH,
+        )
+        copy.start()
+        copies.append(copy)
+    top[...] = jnp.zeros_like(top)
+    bottom[...] = jnp.zeros_like(bottom)
+    west[...] = jnp.zeros_like(west)
+    east[...] = jnp.zeros_like(east)
+    for copy in copies:
+        copy.wait()
+
+    def load(slot, d):
+        other = table[me, d]
+        place = jnp.where(other == count, 0, lax.rem(me - other + count, count))
+        strips[slot] = slots[place].astype(jnp.float32)
+
+    for edge, (left, centre, right) in ((top, (4, 0, 5)), (bottom, (6, 1, 7))):
+        load(0, left)
+        load(1, centre)
+        load(2, right)
+        for k in range(3):
+            edge[k, 5:8] = strips[0, k * side + side - 3 : k * side + side]
+            edge[k, 8 : 8 + side] = strips[1, k * side : k * side + side]
+            edge[k, 8 + side : 11 + side] = strips[2, k * side : k * side + 3]
+    load(0, 2)
+    load(1, 3)
+    for h in range(side):
+        west[h, 5:8] = strips[0, 3 * h : 3 * h + 3]
+        east[h, 0:3] = strips[1, 3 * h : 3 * h + 3]
+
+
+def exchange_rims(tile, table, count, call):
     side, _, channels = tile.shape
-    columns = lambda part: jnp.transpose(part, (1, 0, 2))
-    strips = jnp.stack([tile[-3:], tile[:3], columns(tile[:, -3:]), columns(tile[:, :3])])
-    strips = strips.reshape(4, 3 * side, channels)
-    kinds = jnp.array(kind_of, jnp.int32)
-    slots = [jnp.zeros_like(strips[0])]
-    for offset in range(1, count):
-        peer = lax.rem(me + offset, count)
-        rows = lax.dynamic_index_in_dim(table, peer, 0, keepdims=False)
-        kind = jnp.sum(jnp.where(rows == me, kinds, 0))
-        message = lax.dynamic_index_in_dim(strips, kind, 0, keepdims=False)
-        perm = [(i, (i + offset) % count) for i in range(count)]
-        slots.append(lax.ppermute(message, "tile", perm))
-    slots = jnp.stack(slots).reshape(count, 3, side, channels)
-    mine = lax.dynamic_index_in_dim(table, me, 0, keepdims=False)
-    place = jnp.where(mine == count, 0, lax.rem(me - mine + count, count))
-    strip = [lax.dynamic_index_in_dim(slots, place[d], 0, keepdims=False) for d in range(8)]
-    blank = jnp.zeros((3, 5, channels), tile.dtype)
-
-    def edge(left, centre, right):
-        whole = jnp.concatenate([blank, left[:, -3:], centre, right[:, :3], blank], 1)
-        return whole.astype(jnp.float32)
-
-    top = edge(strip[4], strip[0], strip[5])
-    bottom = edge(strip[6], strip[1], strip[7])
-    west = jnp.pad(columns(strip[2]), ((0, 0), (5, 0), (0, 0))).astype(jnp.float32)
-    east = jnp.pad(columns(strip[3]), ((0, 0), (0, 5), (0, 0))).astype(jnp.float32)
-    return top, bottom, west, east
+    vmem = pl.BlockSpec(memory_space=pltpu.VMEM)
+    edge = jax.ShapeDtypeStruct((3, side + 16, channels), jnp.float32)
+    flank = jax.ShapeDtypeStruct((side, 8, channels), jnp.float32)
+    return pl.pallas_call(
+        functools.partial(rim_body, count),
+        out_shape=(edge, edge, flank, flank),
+        in_specs=[pl.BlockSpec(memory_space=pltpu.SMEM), vmem],
+        out_specs=(vmem,) * 4,
+        scratch_shapes=[
+            pltpu.VMEM((4, 3 * side, channels), jnp.float32),
+            pltpu.VMEM((count - 1, 3 * side, channels), jnp.bfloat16),
+            pltpu.VMEM((count, 3 * side, channels), jnp.bfloat16),
+            pltpu.SemaphoreType.DMA((count - 1,)),
+            pltpu.SemaphoreType.DMA((count - 1,)),
+        ],
+        compiler_params=params(collective_id=call, has_side_effects=True),
+        cost_estimate=pl.CostEstimate(
+            flops=10**9, bytes_accessed=8 << 20, transcendentals=0
+        ),
+        name="rims" + str(call),
+    )(table, tile)
 
 
 def fill(ext, tile_ref, top_ref, bottom_ref, west_ref, east_ref):
@@ -196,6 +254,7 @@
 
 
 def mlp_body(
+    extents,
     conv_ref,
     x_ref,
     g_ref,
@@ -219,10 +278,59 @@
     white,
     branch,
     normed_grad,
+    core_send,
+    core_recv,
+    up_sum,
+    down_sum,
+    up_recv,
+    down_recv,
+    core_sems,
+    up_sems,
+    down_sems,
 ):
     step = pl.program_id(0)
     pixels, channels = conv_ref.shape
     part = 128
+    rest, his, los = extents
+    slide, tile = lax.axis_index("slide"), lax.axis_index("tile")
+    core, hi, lo = lax.rem(slide, 2), tile // los, lax.rem(tile, los)
+    rows = core_send.shape[1] // (his * los)
+    core_peer = {"slide": slide + 1 - 2 * core}
+    hi_peer = {"tile": (1 - hi) * los + lo}
+    lo_next = [lax.rem(lo + offset, los) for offset in range(1, los)]
+    lo_peers = [{"tile": hi * los + other} for other in lo_next]
+
+    def remote(source, target, sems, device):
+        return pltpu.make_async_remote_copy(
+            src_ref=source,
+            dst_ref=target,
+            send_sem=sems[0],
+            recv_sem=sems[1],
+            device_id=device,
+            device_id_type=pl.DeviceIdType.MESH,
+        )
+
+    def core_copy(b):
+        sems = (core_sems.at[0, b], core_sems.at[1, b])
+        return remote(core_send.at[b], core_recv.at[b], sems, core_peer)
+
+    def up_copy(b):
+        sems = (up_sems.at[0, b], up_sems.at[1, b])
+        return remote(up_sum.at[b, 1 - hi], up_recv.at[b], sems, hi_peer)
+
+    def down_copy(b, i):
+        sems = (down_sems.at[0, b, i], down_sems.at[1, b, i])
+        return remote(down_sum.at[b, lo_next[i]], down_recv.at[b, i], sems, lo_peers[i])
+
+    @pl.when(step == 0)
+    def _():
+        barrier = pltpu.get_barrier_semaphore()
+        peers = [core_peer, hi_peer] + lo_peers
+        for peer in peers:
+            pl.semaphore_signal(
+                barrier, inc=1, device_id=peer, device_id_type=pl.DeviceIdType.MESH
+            )
+        pl.semaphore_wait(barrier, len(peers))
 
     @pl.when(step == 0)
     def _():
@@ -246,8 +354,9 @@
         branch[...] = jnp.zeros_like(branch)
         normed_grad[...] = jnp.zeros_like(normed_grad)
 
-    up, down = up_ref[...], down_ref[...]
-    pre = nt(flat[...], up) + up_bias_ref[...]
+    up = up_ref[...]
+    down = down_ref[0] if len(down_ref.shape) == 3 else down_ref[...]
+    pre = nt(flat[...], up) + up_bias_ref[0]
     act_grad = nn(branch_grad[...], down)
     cdf = 0.5 * (1.0 + lax.erf(pre * root_half))
     slope = cdf + pre * inv_root_two_pi * jnp.exp(-0.5 * pre * pre)
@@ -256,9 +365,30 @@
     pre_grad = pre_grad_wide.astype(jnp.bfloat16)
     branch[...] += nt(act, down)
     normed_grad[...] += nn(pre_grad, up)
-    bias_ref[...] = jnp.sum(pre_grad.astype(jnp.float32), axis=0, keepdims=True)
-    up_grad_ref[...] = nn(pre_grad.T, flat[...]).astype(jnp.bfloat16)
-    down_grad_ref[...] = nn(act.T, branch_grad[...]).astype(jnp.bfloat16)
+    bias_ref[0] = jnp.sum(pre_grad.astype(jnp.float32), axis=0, keepdims=True)
+    up_grad = nn(pre_grad.T, flat[...])
+    down_grad = nn(act.T, branch_grad[...])
+
+    @pl.when(step < rest)
+    def _():
+        core_send[step, :, 0:channels] = up_grad.astype(jnp.bfloat16)
+        core_send[step, :, channels : 2 * channels] = down_grad.astype(jnp.bfloat16)
+        core_copy(step).start()
+
+    @pl.when(step >= rest)
+    def _():
+        b = step - rest
+        core_copy(b).wait_recv()
+        up_total = up_grad + core_recv[b, :, 0:channels].astype(jnp.float32)
+        down_total = down_grad + core_recv[b, :, channels : 2 * channels].astype(jnp.float32)
+        for h in range(his):
+            for l in range(los):
+                at = (h * los + l) * rows
+                up_sum[b, h, l] = up_total[at : at + rows].astype(jnp.bfloat16)
+                down_sum[b, l, h] = down_total[at : at + rows].astype(jnp.bfloat16)
+        up_copy(b).start()
+        for i in range(los - 1):
+            down_copy(b, i).start()
 
     @pl.when(step == pl.num_programs(0) - 1)
     def _():
@@ -287,27 +417,57 @@
         sums_ref[1:2, :] = totals[1]
         sums_ref[3:4, :] = totals[2]
 
-
-def mlp(conv, x, g, keep, gain, shift, up, up_bias, down, down_bias, scale):
+        def finish(b, carry):
+            core_copy(b).wait_send()
+            up_copy(b).wait()
+            total = up_sum[b, hi].astype(jnp.float32) + up_recv[b].astype(jnp.float32)
+            up_grad_ref[b] = total.astype(jnp.bfloat16)
+            total = down_sum[b, lo].astype(jnp.float32)
+            for i in range(los - 1):
+                down_copy(b, i).wait()
+                total = total + down_recv[b, i].astype(jnp.float32)
+            down_grad_ref[b] = total.astype(jnp.bfloat16)
+            return carry
+
+        lax.fori_loop(0, rest, finish, 0)
+
+
+def mlp(conv, x, g, keep, gain, shift, up, up_bias, down, down_bias, scale, slides, tiles):
     pixels, channels = conv.shape
     hidden = up.shape[0]
-    block = 256
+    rest, his, los = slides // 2, 2, tiles // 2
+    blocks = 2 * rest
+    block = hidden // blocks
+    rows = block // tiles
+    single = pl.Buffered(buffer_count=1)
     whole = lambda shape: pl.BlockSpec(
-        shape, lambda j: (0, 0), pipeline_mode=pl.Buffered(buffer_count=1)
+        shape, lambda j: (0,) * len(shape), pipeline_mode=single
     )
-    full = lambda shape: pl.BlockSpec(shape, lambda j: (0, 0))
     row = pl.BlockSpec((1, channels), lambda j: (0, 0))
+
+    def at(j):
+        core = lax.rem(lax.axis_index("slide"), 2)
+        return lax.rem(j, rest) * 2 + jnp.where(j < rest, 1 - core, core)
+
+    if block % lanes == 0:
+        down_spec = pl.BlockSpec((channels, block), lambda j: (0, at(j)))
+    else:
+        down = jnp.transpose(down.reshape(channels, blocks, block), (1, 0, 2))
+        down_spec = pl.BlockSpec((1, channels, block), lambda j: (at(j), 0, 0))
+    bias_spec = pl.BlockSpec((1, 1, block), lambda j: (at(j), 0, 0))
+    shape = jax.ShapeDtypeStruct
+    wide, narrow = jnp.float32, jnp.bfloat16
     return pl.pallas_call(
-        mlp_body,
+        functools.partial(mlp_body, (rest, his, los)),
         out_shape=(
-            jax.ShapeDtypeStruct((pixels, channels), jnp.bfloat16),
-            jax.ShapeDtypeStruct((pixels, channels), jnp.bfloat16),
-            jax.ShapeDtypeStruct((hidden, channels), jnp.bfloat16),
-            jax.ShapeDtypeStruct((hidden, channels), jnp.bfloat16),
-            jax.ShapeDtypeStruct((4, channels), jnp.float32),
-            jax.ShapeDtypeStruct((1, hidden), jnp.float32),
+            shape((pixels, channels), narrow),
+            shape((pixels, channels), narrow),
+            shape((rest, los, rows, channels), narrow),
+            shape((rest, his, rows, channels), narrow),
+            shape((4, channels), wide),
+            shape((blocks, 1, block), wide),
         ),
-        grid=(hidden // block,),
+        grid=(blocks,),
         in_specs=[
             whole((pixels, channels)),
             whole((pixels, channels)),
@@ -315,36 +475,45 @@
             pl.BlockSpec((1, lanes), lambda j: (0, 0)),
             row,
             row,
-            pl.BlockSpec((block, channels), lambda j: (j, 0)),
-            pl.BlockSpec((1, block), lambda j: (0, j)),
-            pl.BlockSpec((channels, block), lambda j: (0, j)),
+            pl.BlockSpec((block, channels), lambda j: (at(j), 0)),
+            bias_spec,
+            down_spec,
             row,
             row,
         ],
         out_specs=(
-            full((pixels, channels)),
-            full((pixels, channels)),
-            pl.BlockSpec((block, channels), lambda j: (j, 0)),
-            pl.BlockSpec((block, channels), lambda j: (j, 0)),
+            whole((pixels, channels)),
+            whole((pixels, channels)),
+            whole((rest, los, rows, channels)),
+            whole((rest, his, rows, channels)),
             pl.BlockSpec((4, channels), lambda j: (0, 0)),
-            pl.BlockSpec((1, block), lambda j: (0, j)),
+            bias_spec,
         ),
         scratch_shapes=[
-            pltpu.VMEM((pixels, channels), jnp.bfloat16),
-            pltpu.VMEM((pixels, channels), jnp.bfloat16),
-            pltpu.VMEM((pixels, lanes), jnp.float32),
-            pltpu.VMEM((pixels, channels), jnp.float32),
-            pltpu.VMEM((pixels, channels), jnp.float32),
-            pltpu.VMEM((pixels, channels), jnp.float32),
+            pltpu.VMEM((pixels, channels), narrow),
+            pltpu.VMEM((pixels, channels), narrow),
+            pltpu.VMEM((pixels, lanes), wide),
+            pltpu.VMEM((pixels, channels), wide),
+            pltpu.VMEM((pixels, channels), wide),
+            pltpu.VMEM((pixels, channels), wide),
+            pltpu.VMEM((rest, block, 2 * channels), narrow),
+            pltpu.VMEM((rest, block, 2 * channels), narrow),
+            pltpu.VMEM((rest, his, los, rows, channels), narrow),
+            pltpu.VMEM((rest, los, his, rows, channels), narrow),
+            pltpu.VMEM((rest, los, rows, channels), narrow),
+            pltpu.VMEM((rest, los - 1, his, rows, channels), narrow),
+            pltpu.SemaphoreType.DMA((2, rest)),
+            pltpu.SemaphoreType.DMA((2, rest)),
+            pltpu.SemaphoreType.DMA((2, rest, los - 1)),
         ],
-        compiler_params=params(),
+        compiler_params=params(collective_id=2, has_side_effects=True),
         cost_estimate=pl.CostEstimate(
             flops=12 * pixels * channels * hidden,
             bytes_accessed=32 << 20,
             transcendentals=2 * pixels * hidden,
         ),
         name="mlp",
-    )(conv, x, g, keep, gain, shift, up, up_bias, down, down_bias, scale)
+    )(conv, x, g, keep, gain, shift, up, up_bias.reshape(blocks, 1, block), down, down_bias, scale)
 
 
 class Grid:
@@ -413,14 +582,13 @@
     slides, tiles = lax.axis_size("slide"), lax.axis_size("tile")
     side, channels = features.shape[3], features.shape[4]
     hidden = up_weight.shape[1]
-    me = lax.axis_index("tile")
     table = neighbours[0]
     grid = Grid(slides, tiles)
     tile, grad = features[0, 0], cotangent[0, 0]
     taps = dw_weight[0].reshape(49, channels)
     keep = jnp.broadcast_to((1 - skip_flags[0, 0]).astype(jnp.float32), (1, lanes))
 
-    rims = exchange_rims(tile, table, me, tiles)
+    rims = exchange_rims(tile, table, tiles, 0)
     conv = depthwise(tile, rims, taps)
     block_out, conv_grad, up_grad, down_grad, sums, bias = mlp(
         conv.reshape(-1, channels),
@@ -434,17 +602,14 @@
         down_weight[0],
         down_bias,
         layer_scale,
+        slides,
+        tiles,
     )
     conv_tile = conv_grad.reshape(side, side, channels)
-    grad_rims = exchange_rims(conv_tile, table, me, tiles)
-
-    shape = tuple(grid.sizes[n] for n in grid.names)
-    up_part = grid.scatter(up_grad.reshape(*shape, -1, channels), 1, "core")
-    down_part = grid.scatter(down_grad.reshape(*shape, -1, channels), 1, "core")
-    up_part = grid.scatter(up_part, 1, "hi")
-    down_part = grid.scatter(down_part, 2, "lo")
-    up_part = grid.scatter(up_part, 1, "lo")
-    down_part = grid.scatter(down_part, 1, "hi")
+    grad_rims = exchange_rims(conv_tile, table, tiles, 1)
+
+    up_part = grid.scatter(up_grad, 1, "lo")
+    down_part = grid.scatter(down_grad, 1, "hi")
     up_part = grid.scatter(up_part, 0, "rest", last=True)
     down_part = grid.scatter(down_part, 0, "rest", last=True)
     weight_grads = jnp.concatenate([up_part, down_part], -1)[None]

time: 230 us -> 210 us (0.913)
  Pallas kernels: 97.3 us -> 146 us
  between operations: 23.1 us -> 1.5 us
  local copies, waits for them, and re-layouts: 22.9 us -> 7.29 us
  other arithmetic: 21.1 us -> 7.73 us
  starting transfers between devices: 27.2 us -> 14.4 us
  waiting for transfers between devices: 37.9 us -> 32.7 us
    pallas_call x1 -> x3, Pallas kernels: 47.5 us -> 95.8 us  [the longest x1 62 us: mlp(): pl.pallas_call(functools.partial(mlp_body, (rest, his, los)), out_shape=(...]
    dynamic_slice x8 -> x0, local copies, waits for them, and re-layouts: 8.3 us -> none  [the longest x4 7.85 us: scatter(): pick = lambda i: lax.dynamic_index_in_dim(value, i, dim, keepdims=False)]
    ppermute x6 -> x0, starting transfers between devices: 8.06 us -> none  [exchange_rims(): slots.append(lax.ppermute(message, 'tile', perm))]
    convert_element_type x8 -> x0, other arithmetic: 7.09 us -> none  [the longest x4 3.2 us: edge(): return whole.astype(jnp.float32)]
    convert_element_type x6 -> x2, other arithmetic: 8.34 us -> 2.4 us  [scatter(): return total if last else total.astype(jnp.bfloat16)]
    ppermute x17 -> x13, starting transfers between devices: 19.1 us -> 14.4 us  [send(): return lax.ppermute(value, ('slide', 'tile'), self.perm(axis, move))]
    ppermute x6 -> x0, waiting for transfers between devices: 3.72 us -> none  [exchange_rims(): slots.append(lax.ppermute(message, 'tile', perm))]
    transpose x7 -> x0, local copies, waits for them, and re-layouts: 2.88 us -> none  [exchange_rims(): columns = lambda part: jnp.transpose(part, (1, 0, 2))]
  transfers between devices with their start and end apart: 23 -> 13, of which waited for: 9 -> 6; matrix products, arithmetic and copies ran while one was open for 12% -> 4% of each run, Pallas kernels for 14% -> 17%
where the time goes in v2:
time: 210 us; the launch traced here: 209 us
  Pallas kernels  146 us (70%)
  waiting for transfers between devices  32.7 us (16%)
  starting transfers between devices  14.4 us (7%)
  other arithmetic  7.73 us (4%)
  local copies, waits for them, and re-layouts  7.29 us (3%)
    pallas_call x1, Pallas kernels, mlp(): pl.pallas_call(functools.partial(mlp_body, (rest, his, los)), out_shape=(...  62 us
    pallas_call x2, Pallas kernels, exchange_rims(): pl.pallas_call(functools.partial(rim_body, count), out_shape=(edge, edge,...  33.8 us
    pallas_call x2, Pallas kernels, depthwise(): pl.pallas_call(functools.partial(conv_body, add is not None), out_shape=o...  33.4 us
    ppermute x13, waiting for transfers between devices, send(): return lax.ppermute(value, ('slide', 'tile'), self.perm(axis, move))  32.7 us
    pallas_call x1, Pallas kernels, kernel_grad(): pl.pallas_call(kernel_grad_body, out_shape=jax.ShapeDtypeStruct((49, chan...  16.4 us
    ppermute x13, starting transfers between devices, send(): return lax.ppermute(value, ('slide', 'tile'), self.perm(axis, move))  14.4 us
  transfers between devices with their start and end apart: 13, of which 6 were waited for; matrix products, arithmetic and copies ran while one was open for 4% of the time, Pallas kernels for 17%

profile of v2, /device:TPU:0, one launch (start us, length us, event | category | flops | bytes accessed | tf_op | source)
XLA Modules:
  0.0 209.2 jit_solution(7938620549150735622)
XLA Ops:
  0.6 1.3 reduce
  1.9 0.7 reshape_squeeze.9.weight_ref
  3.3 14.3 %rims0.1 = (f32[3,48,768]{2,1,0:T(8,128)}, f32[3,48,768]{2,1,0:T(8,128)}, f32[32,8,768]{2,1,0:T(8,128)}, f32[32,8,768]{2,1,0:T(8,128)}) custom-call(s32[4,8]{1,0:T(4,128)} %bitcast.60, bf16[32,32,768]{2,1,0:T(8,128)(2,1)} %bitcast.53), custom_call_target="tpu_custom_call" | custom-call | flops 1000000000 | bytes 8388608 | tf_op jit(solution)/shard_map/rims0/pallas_call | solution.py:92
  17.6 16.7 %depthwise.2 = f32[32,32,768]{2,1,0:T(8,128)} custom-call(bf16[32,32,768]{2,1,0:T(8,128)(2,1)} %bitcast.54, f32[3,48,768]{2,1,0:T(8,128)} %get-tuple-element.20.top, f32[3,48,768]{2,1,0:T(8,128)} %get-tuple-element.21.bottom, f32[32,8,768]{2,1,0:T(8,128)} %get-tuple-element.22.west, f32[32,8,768]{2,1,0:T(8,128)} %get-tuple-element.23.east, ...), custom_call_target="tpu_custom_call" | custom-call | flops 7707033600 | bytes 8388608 | tf_op jit(solution)/shard_map/depthwise/pallas_call | solution.py:173
  34.3 0.5 broadcast_in_dim.12.keep_ref
  34.8 62.0 %mlp.1 = (bf16[1024,768]{1,0:T(8,128)(2,1)}, bf16[1024,768]{1,0:T(8,128)(2,1)}, bf16[4,2,96,768]{3,2,1,0:T(8,128)(2,1)}, bf16[4,2,96,768]{3,2,1,0:T(8,128)(2,1)}...) custom-call(f32[1024,768]{1,0:T(8,128)} %bitcast.62, bf16[1024,768]{1,0:T(8,128)(2,1)} %bitcast.55, bf16[1024,768]{1,0:T(8,128)(2,1)} %bitcast.57, ...), custom_call_target="tpu_custom_call" | custom-call | flops 28991029248 | bytes 33554432 | tf_op jit(solution)/shard_map/mlp/pallas_call | solution.py:460
  96.8 0.0 copy-start.6
  96.8 0.0 copy-start.5
  96.8 0.0 copy-start.2
  96.8 16.4 %kernel_grad.1 = f32[49,768]{1,0:T(8,128)} custom-call(bf16[32,32,768]{2,1,0:T(8,128)(2,1)} %bitcast.56, f32[3,48,768]{2,1,0:T(8,128)} %get-tuple-element.20.top, f32[3,48,768]{2,1,0:T(8,128)} %get-tuple-element.21.bottom, f32[32,8,768]{2,1,0:T(8,128)} %get-tuple-element.22.west, f32[32,8,768]{2,1,0:T(8,128)} %get-tuple-element.23.east, ...), custom_call_target="tpu_custom_call" | custom-call | flops 7707033600 | bytes 8388608 | tf_op jit(solution)/shard_map/kernel_grad/pallas_call | solution.py:229
  113.2 0.0 copy-start.4
  113.2 0.0 copy-start.1
  113.2 0.0 copy-done.6
  113.3 0.0 copy-done.5
  113.3 1.0 pad_maximum_fusion
  114.3 1.5 collective-permute-start.8
  115.8 0.0 copy-done.2
  115.9 0.0 copy-start.3
  115.9 0.6 collective-permute-start
  116.5 5.8 %collective-permute-done.8 = f32[57,768]{1,0:T(8,128)} collective-permute-done((f32[57,768]{1,0:T(8,128)S(1)}, f32[57,768]{1,0:T(8,128)}, u32[]{:S(2)}, u32[]{:S(2)}) %collective-permute-start.8) | collective-permute-done | bytes 175136 | tf_op jit(solution)/shard_map/ppermute | solution.py:547
  122.3 0.0 copy-done.4
  122.3 1.0 fusion.6
  123.3 1.4 collective-permute-start.9
  124.7 0.0 copy-done.1
  124.7 0.9 dynamic-slice_bitcast_fusion
  125.6 0.7 collective-permute-start.4
  126.3 0.0 copy-done.3
  126.3 1.9 rev.3.weight_ref
  128.1 19.4 %rims1.1 = (f32[3,48,768]{2,1,0:T(8,128)}, f32[3,48,768]{2,1,0:T(8,128)}, f32[32,8,768]{2,1,0:T(8,128)}, f32[32,8,768]{2,1,0:T(8,128)}) custom-call(s32[4,8]{1,0:T(4,128)} %bitcast.61, bf16[32,32,768]{2,1,0:T(8,128)(2,1)} %bitcast.65), custom_call_target="tpu_custom_call" | custom-call | flops 1000000000 | bytes 8388608 | tf_op jit(solution)/shard_map/rims1/pallas_call | solution.py:92
  147.6 0.0 collective-permute-done.9
  147.6 0.9 add.111
  148.6 0.1 collective-permute-start.10
  148.6 16.7 %depthwise.3 = bf16[32,32,768]{2,1,0:T(8,128)(2,1)} custom-call(bf16[32,32,768]{2,1,0:T(8,128)(2,1)} %bitcast.66, f32[3,48,768]{2,1,0:T(8,128)} %get-tuple-element.26.top, f32[3,48,768]{2,1,0:T(8,128)} %get-tuple-element.27.bottom, f32[32,8,768]{2,1,0:T(8,128)} %get-tuple-element.28.west, f32[32,8,768]{2,1,0:T(8,128)} %get-tuple-element.29.east, ...), custom_call_target="tpu_custom_call" | custom-call | flops 7707033600 | bytes 8388608 | tf_op jit(solution)/shard_map/depthwise/pallas_call | solution.py:173
  165.4 0.0 collective-permute-done.10
  165.4 1.7 collective-permute-start.11
  167.1 0.0 collective-permute-done
  167.1 1.2 fusion.1
  168.3 0.5 collective-permute-start.1
  168.8 2.6 %collective-permute-start.2 = (bf16[96,768]{1,0:T(8,128)(2,1)S(1)}, bf16[96,768]{1,0:T(8,128)(2,1)S(1)}, u32[]{:S(2)}, u32[]{:S(2)}) collective-permute-start(bf16[96,768]{1,0:T(8,128)(2,1)S(1)} %get-tuple-element.48), channel_id=1, source_target_pairs={{0,16},{1,17},{2,18},{3,19},{4,20},{5,21},{6,22},{7,23},{8,24},{9,... | collective-permute-start | bytes 442376 | tf_op jit(solution)/shard_map/ppermute | solution.py:547
  171.4 2.5 %collective-permute-start.3 = (bf16[96,768]{1,0:T(8,128)(2,1)S(1)}, bf16[96,768]{1,0:T(8,128)(2,1)S(1)}, u32[]{:S(2)}, u32[]{:S(2)}) collective-permute-start(bf16[96,768]{1,0:T(8,128)(2,1)S(1)} %get-tuple-element.47), channel_id=1, source_target_pairs={{0,24},{1,25},{2,26},{3,27},{4,28},{5,29},{6,30},{7,31},{8,0},{9,1... | collective-permute-start | bytes 442376 | tf_op jit(solution)/shard_map/ppermute | solution.py:547
  173.9 0.0 collective-permute-done.4
  173.9 1.2 fusion
  175.1 0.1 collective-permute-start.5
  175.2 3.5 %collective-permute-done.11 = f32[57,768]{1,0:T(8,128)S(1)} collective-permute-done((f32[57,768]{1,0:T(8,128)S(1)}, f32[57,768]{1,0:T(8,128)S(1)}, u32[]{:S(2)}, u32[]{:S(2)}) %collective-permute-start.11) | collective-permute-done | bytes 175136 | tf_op jit(solution)/shard_map/ppermute | solution.py:547
  178.7 0.0 collective-permute-start.6
  178.7 0.0 collective-permute-done.1
  178.8 2.8 %collective-permute-start.7 = (bf16[96,768]{1,0:T(8,128)(2,1)S(1)}, bf16[96,768]{1,0:T(8,128)(2,1)S(1)}, u32[]{:S(2)}, u32[]{:S(2)}) collective-permute-start(bf16[96,768]{1,0:T(8,128)(2,1)S(1)} %get-tuple-element.50), channel_id=1, source_target_pairs={{0,24},{1,25},{2,26},{3,27},{4,28},{5,29},{6,30},{7,31},{8,0},{9,1... | collective-permute-start | bytes 442376 | tf_op jit(solution)/shard_map/ppermute | solution.py:547
  181.5 1.2 collective-permute-done.2
  182.8 0.0 collective-permute-start.12
  182.8 0.0 collective-permute-done.3
  182.8 0.1 fusion.5
  182.8 5.2 %collective-permute-done.5 = bf16[96,768]{1,0:T(8,128)(2,1)S(1)} collective-permute-done((bf16[96,768]{1,0:T(8,128)(2,1)S(1)}, bf16[96,768]{1,0:T(8,128)(2,1)S(1)}, u32[]{:S(2)}, u32[]{:S(2)}) %collective-permute-start.5) | collective-permute-done | bytes 147488 | tf_op jit(solution)/shard_map/ppermute | solution.py:547
  188.0 11.6 %collective-permute-done.6 = bf16[96,768]{1,0:T(8,128)(2,1)S(1)} collective-permute-done((bf16[96,768]{1,0:T(8,128)(2,1)S(1)}, bf16[96,768]{1,0:T(8,128)(2,1)S(1)}, u32[]{:S(2)}, u32[]{:S(2)}) %collective-permute-start.6) | collective-permute-done | bytes 147488 | tf_op jit(solution)/shard_map/ppermute | solution.py:547
  199.6 0.0 collective-permute-done.7
  199.6 0.1 fusion.3
  199.7 0.0 copy-start
  199.7 0.9 maximum_bitcast_fusion
  200.6 5.4 %collective-permute-done.12 = f32[57,768]{1,0:T(8,128)S(1)} collective-permute-done((f32[57,768]{1,0:T(8,128)S(1)}, f32[57,768]{1,0:T(8,128)S(1)}, u32[]{:S(2)}, u32[]{:S(2)}) %collective-permute-start.12) | collective-permute-done | bytes 175136 | tf_op jit(solution)/shard_map/ppermute | solution.py:547
  206.0 0.6 slice_bitcast_fusion
  206.6 0.8 reshape.55
  207.4 0.6 copy.23
  208.0 0.0 copy-done
  208.0 1.1 copy.28
  (9 shorter events, 0.2 us)
Async XLA Ops:
  96.8 16.4 %copy-start.6 = (f32[8,1,384]{2,1,0:T(1,128)S(1)}, f32[8,1,384]{2,1,0:T(1,128)}, u32[]{:S(2)}) copy-start(f32[8,1,384]{2,1,0:T(1,128)} %get-tuple-element.33) | copy-start | bytes 36868
  96.8 16.4 %copy-start.5 = (f32[4,768]{1,0:T(4,128)S(1)}, f32[4,768]{1,0:T(4,128)}, u32[]{:S(2)}) copy-start(f32[4,768]{1,0:T(4,128)} %get-tuple-element.32) | copy-start | bytes 36868
  96.8 19.0 %copy-start.2 = (bf16[4,2,96,768]{3,2,1,0:T(8,128)(2,1)S(1)}, bf16[4,2,96,768]{3,2,1,0:T(8,128)(2,1)}, u32[]{:S(2)}) copy-start(bf16[4,2,96,768]{3,2,1,0:T(8,128)(2,1)} %get-tuple-element.30) | copy-start | bytes 3538948
  113.2 9.1 %copy-start.4 = (f32[49,768]{1,0:T(8,128)S(1)}, f32[49,768]{1,0:T(8,128)}, u32[]{:S(2)}) copy-start(f32[49,768]{1,0:T(8,128)} %kernel_grad.1) | copy-start | bytes 451588
  113.2 11.5 %copy-start.1 = (bf16[4,2,96,768]{3,2,1,0:T(8,128)(2,1)S(1)}, bf16[4,2,96,768]{3,2,1,0:T(8,128)(2,1)}, u32[]{:S(2)}) copy-start(bf16[4,2,96,768]{3,2,1,0:T(8,128)(2,1)} %get-tuple-element.31) | copy-start | bytes 3538948
  114.3 8.0 %collective-permute-start.8 = (f32[57,768]{1,0:T(8,128)S(1)}, f32[57,768]{1,0:T(8,128)}, u32[]{:S(2)}, u32[]{:S(2)}) collective-permute-start(f32[57,768]{1,0:T(8,128)S(1)} %pad_maximum_fusion), channel_id=1, source_target_pairs={{0,1},{1,0},{2,3},{3,2},{4,5},{5,4},{6,7},{7,6},{8,9},{9,8},{10,11... | collective-permute-start | bytes 525320 | tf_op jit(solution)/shard_map/ppermute | solution.py:547
  115.9 10.4 %copy-start.3 = (f32[49,768]{1,0:T(8,128)S(1)}, f32[49,768]{1,0:T(8,128)}, u32[]{:S(2)}) copy-start(f32[49,768]{1,0:T(8,128)} %reshape_squeeze.9.weight_ref) | copy-start | bytes 451588
  115.9 51.2 %collective-permute-start = (bf16[4,96,768]{2,1,0:T(8,128)(2,1)S(1)}, bf16[4,96,768]{2,1,0:T(8,128)(2,1)}, u32[]{:S(2)}, u32[]{:S(2)}) collective-permute-start(bf16[4,96,768]{2,1,0:T(8,128)(2,1)S(1)} %dynamic-slice_bitcast_fusion.1), channel_id=1, source_target_pairs={{0,1},{1,0},{2,3},{3,2},{4,5},{5,4},{6,7},{7,6},{8,9},{9,8},{10,11... | collective-permute-start | bytes 1769480 | tf_op jit(solution)/shard_map/ppermute | solution.py:547
  123.3 24.3 %collective-permute-start.9 = (f32[57,768]{1,0:T(8,128)S(1)}, f32[57,768]{1,0:T(8,128)}, u32[]{:S(2)}, u32[]{:S(2)}) collective-permute-start(f32[57,768]{1,0:T(8,128)S(1)} %fusion.6), channel_id=1, source_target_pairs={{0,2},{1,3},{2,0},{3,1},{4,6},{5,7},{6,4},{7,5},{8,10},{9,11},{10,... | collective-permute-start | bytes 525320 | tf_op jit(solution)/shard_map/ppermute | solution.py:547
  125.6 48.3 %collective-permute-start.4 = (bf16[4,96,768]{2,1,0:T(8,128)(2,1)}, bf16[4,96,768]{2,1,0:T(8,128)(2,1)}, u32[]{:S(2)}, u32[]{:S(2)}) collective-permute-start(bf16[4,96,768]{2,1,0:T(8,128)(2,1)} %dynamic-slice_bitcast_fusion), channel_id=1, source_target_pairs={{0,2},{1,3},{2,0},{3,1},{4,6},{5,7},{6,4},{7,5},{8,10},{9,11},{10,... | collective-permute-start | bytes 1769480 | tf_op jit(solution)/shard_map/ppermute | solution.py:547
  148.6 16.8 %collective-permute-start.10 = (f32[57,768]{1,0:T(8,128)S(1)}, f32[57,768]{1,0:T(8,128)S(1)}, u32[]{:S(2)}, u32[]{:S(2)}) collective-permute-start(f32[57,768]{1,0:T(8,128)S(1)} %add.111), channel_id=1, source_target_pairs={{0,4},{1,5},{2,6},{3,7},{4,0},{5,1},{6,2},{7,3},{8,12},{9,13},{10,... | collective-permute-start | bytes 525320 | tf_op jit(solution)/shard_map/ppermute | solution.py:547
  165.4 13.3 %collective-permute-start.11 = (f32[57,768]{1,0:T(8,128)S(1)}, f32[57,768]{1,0:T(8,128)S(1)}, u32[]{:S(2)}, u32[]{:S(2)}) collective-permute-start(f32[57,768]{1,0:T(8,128)S(1)} %add.112), channel_id=1, source_target_pairs={{0,8},{1,9},{2,10},{3,11},{4,12},{5,13},{6,14},{7,15},{8,0},{9,1},... | collective-permute-start | bytes 525320 | tf_op jit(solution)/shard_map/ppermute | solution.py:547
  168.3 10.4 %collective-permute-start.1 = (bf16[96,768]{1,0:T(8,128)(2,1)S(1)}, bf16[96,768]{1,0:T(8,128)(2,1)S(1)}, u32[]{:S(2)}, u32[]{:S(2)}) collective-permute-start(bf16[96,768]{1,0:T(8,128)(2,1)S(1)} %get-tuple-element.46), channel_id=1, source_target_pairs={{0,8},{1,9},{2,10},{3,11},{4,12},{5,13},{6,14},{7,15},{8,16},{9,17... | collective-permute-start | bytes 442376 | tf_op jit(solution)/shard_map/ppermute | solution.py:547
  168.8 13.9 %collective-permute-start.2 = (bf16[96,768]{1,0:T(8,128)(2,1)S(1)}, bf16[96,768]{1,0:T(8,128)(2,1)S(1)}, u32[]{:S(2)}, u32[]{:S(2)}) collective-permute-start(bf16[96,768]{1,0:T(8,128)(2,1)S(1)} %get-tuple-element.48), channel_id=1, source_target_pairs={{0,16},{1,17},{2,18},{3,19},{4,20},{5,21},{6,22},{7,23},{8,24},{9,... | collective-permute-start | bytes 442376 | tf_op jit(solution)/shard_map/ppermute | solution.py:547
  171.4 11.4 %collective-permute-start.3 = (bf16[96,768]{1,0:T(8,128)(2,1)S(1)}, bf16[96,768]{1,0:T(8,128)(2,1)S(1)}, u32[]{:S(2)}, u32[]{:S(2)}) collective-permute-start(bf16[96,768]{1,0:T(8,128)(2,1)S(1)} %get-tuple-element.47), channel_id=1, source_target_pairs={{0,24},{1,25},{2,26},{3,27},{4,28},{5,29},{6,30},{7,31},{8,0},{9,1... | collective-permute-start | bytes 442376 | tf_op jit(solution)/shard_map/ppermute | solution.py:547
  175.1 12.9 %collective-permute-start.5 = (bf16[96,768]{1,0:T(8,128)(2,1)S(1)}, bf16[96,768]{1,0:T(8,128)(2,1)S(1)}, u32[]{:S(2)}, u32[]{:S(2)}) collective-permute-start(bf16[96,768]{1,0:T(8,128)(2,1)S(1)} %get-tuple-element.49), channel_id=1, source_target_pairs={{0,8},{1,9},{2,10},{3,11},{4,12},{5,13},{6,14},{7,15},{8,16},{9,17... | collective-permute-start | bytes 442376 | tf_op jit(solution)/shard_map/ppermute | solution.py:547
  178.7 20.9 %collective-permute-start.6 = (bf16[96,768]{1,0:T(8,128)(2,1)S(1)}, bf16[96,768]{1,0:T(8,128)(2,1)S(1)}, u32[]{:S(2)}, u32[]{:S(2)}) collective-permute-start(bf16[96,768]{1,0:T(8,128)(2,1)S(1)} %get-tuple-element.51), channel_id=1, source_target_pairs={{0,16},{1,17},{2,18},{3,19},{4,20},{5,21},{6,22},{7,23},{8,24},{9,... | collective-permute-start | bytes 442376 | tf_op jit(solution)/shard_map/ppermute | solution.py:547
  178.8 20.8 %collective-permute-start.7 = (bf16[96,768]{1,0:T(8,128)(2,1)S(1)}, bf16[96,768]{1,0:T(8,128)(2,1)S(1)}, u32[]{:S(2)}, u32[]{:S(2)}) collective-permute-start(bf16[96,768]{1,0:T(8,128)(2,1)S(1)} %get-tuple-element.50), channel_id=1, source_target_pairs={{0,24},{1,25},{2,26},{3,27},{4,28},{5,29},{6,30},{7,31},{8,0},{9,1... | collective-permute-start | bytes 442376 | tf_op jit(solution)/shard_map/ppermute | solution.py:547
  182.8 23.2 %collective-permute-start.12 = (f32[57,768]{1,0:T(8,128)S(1)}, f32[57,768]{1,0:T(8,128)S(1)}, u32[]{:S(2)}, u32[]{:S(2)}) collective-permute-start(f32[57,768]{1,0:T(8,128)S(1)} %add.113), channel_id=1, source_target_pairs={{0,16},{1,17},{2,18},{3,19},{4,20},{5,21},{6,22},{7,23},{8,24},{9,... | collective-permute-start | bytes 525320 | tf_op jit(solution)/shard_map/ppermute | solution.py:547
  199.7 8.4 %copy-start = (bf16[1024,768]{1,0:T(8,128)(2,1)S(1)}, bf16[1024,768]{1,0:T(8,128)(2,1)}, u32[]{:S(2)}) copy-start(bf16[1024,768]{1,0:T(8,128)(2,1)} %get-tuple-element.24) | copy-start | bytes 4718596

commit v3 on v2

--- a/solution.py
+++ b/solution.py
@@ -103,7 +103,7 @@
         ],
         compiler_params=params(collective_id=call, has_side_effects=True),
         cost_estimate=pl.CostEstimate(
-            flops=10**9, bytes_accessed=8 << 20, transcendentals=0
+            flops=10**10, bytes_accessed=8 << 20, transcendentals=0
         ),
         name="rims" + str(call),
     )(table, tile)
@@ -118,11 +118,12 @@
     ext[3 : side + 3, side + 8 : side + 16] = east_ref[...]
 
 
-def conv_body(with_add, tile_ref, top, bottom, west, east, weight_ref, *rest):
-    if with_add:
-        add_ref, out_ref, ext, shifted, total = rest
-    else:
-        out_ref, ext, shifted, total = rest
+def conv_body(tile_ref, top, bottom, west, east, weight_ref, out_ref, ext, shifted, total):
+    conv_sum(tile_ref, top, bottom, west, east, weight_ref, ext, shifted, total)
+    out_ref[...] = total[...]
+
+
+def conv_sum(tile_ref, top, bottom, west, east, weight_ref, ext, shifted, total):
     side = tile_ref.shape[0]
     fill(ext, tile_ref, top, bottom, west, east)
     for b in range(7):
@@ -155,34 +156,204 @@
             return carry
 
         lax.fori_loop(0, side // row_step, rows, 0)
-    if with_add:
-        out_ref[...] = (add_ref[...].astype(jnp.float32) + total[...]).astype(jnp.bfloat16)
-    else:
-        out_ref[...] = total[...]
+
+
+def back_body(
+    extents,
+    tile_ref,
+    top,
+    bottom,
+    west,
+    east,
+    weight_ref,
+    add_ref,
+    up,
+    down,
+    small,
+    out_ref,
+    up_out,
+    down_out,
+    small_out,
+    ext,
+    shifted,
+    total,
+    up_recv,
+    down_recv,
+    small_recv,
+    slide_slots,
+    tile_slots,
+    up_sems,
+    down_sems,
+    small_sems,
+    slide_sems,
+    tile_sems,
+):
+    slides, tiles = extents
+    rest = slides // 2
+    step = pl.program_id(0)
+    slide, tile = lax.axis_index("slide"), lax.axis_index("tile")
+    far, core = slide // 2, lax.rem(slide, 2)
+    next_tile = [lax.rem(tile + o, tiles) for o in range(1, tiles)]
+    next_slide = [lax.rem(slide + o, slides) for o in range(1, slides)]
+    next_far = [lax.rem(far + o, rest) for o in range(1, rest)]
+
+    def remote(source, target, sems, i, device):
+        return pltpu.make_async_remote_copy(
+            src_ref=source,
+            dst_ref=target,
+            send_sem=sems.at[0, i],
+            recv_sem=sems.at[1, i],
+            device_id=device,
+            device_id_type=pl.DeviceIdType.MESH,
+        )
+
+    def far_copies(part, recv, sems):
+        return [
+            remote(part.at[at], recv.at[i], sems, i, {"slide": at * 2 + core})
+            for i, at in enumerate(next_far)
+        ]
+
+    def small_copies():
+        return [
+            remote(small.at[at], small_recv.at[i], small_sems, i, {"tile": at})
+            for i, at in enumerate(next_tile)
+        ]
+
+    def slide_copies():
+        return [
+            remote(slide_slots.at[0], slide_slots.at[i + 1], slide_sems, i, {"slide": at})
+            for i, at in enumerate(next_slide)
+        ]
+
+    def tile_copies():
+        return [
+            remote(tile_slots.at[0], tile_slots.at[i + 1], tile_sems, i, {"tile": at})
+            for i, at in enumerate(next_tile)
+        ]
+
+    @pl.when(step == 0)
+    def _():
+        barrier = pltpu.get_barrier_semaphore()
+        peers = [{"tile": at} for at in next_tile] + [{"slide": at} for at in next_slide]
+        for peer in peers:
+            pl.semaphore_signal(
+                barrier, inc=1, device_id=peer, device_id_type=pl.DeviceIdType.MESH
+            )
+        pl.semaphore_wait(barrier, len(peers))
+        for copy in small_copies() + far_copies(up, up_recv, up_sems):
+            copy.start()
+
+    @pl.when(step == 1)
+    def _():
+        own = small[tile]
+        for i, copy in enumerate(small_copies()):
+            copy.wait()
+            own = own + small_recv[i]
+        slide_slots[0] = own
+        for copy in slide_copies() + far_copies(down, down_recv, down_sems):
+            copy.start()
+
+    @pl.when(step == 4)
+    def _():
+        for copy in slide_copies():
+            copy.wait()
+        own = slide_slots[lax.rem(slide, slides)]
+        for i in range(1, slides):
+            own = own + slide_slots[lax.rem(slide - i + slides, slides)]
+        tile_slots[0] = own
+        for copy in tile_copies():
+            copy.start()
+
+    conv_sum(tile_ref, top, bottom, west, east, weight_ref, ext, shifted, total)
+    out_ref[...] = (add_ref[...].astype(jnp.float32) + total[...]).astype(jnp.bfloat16)
+
+    @pl.when(step == pl.num_programs(0) - 1)
+    def _():
+        for copy in tile_copies():
+            copy.wait()
+        for i in range(tiles):
+            small_out[i] = tile_slots[lax.rem(tile - i + tiles, tiles)]
+        for part, recv, sems, out in (
+            (up, up_recv, up_sems, up_out),
+            (down, down_recv, down_sems, down_out),
+        ):
+            out[...] = part[far].astype(jnp.float32)
+            for i, copy in enumerate(far_copies(part, recv, sems)):
+                copy.wait()
+                out[...] += recv[i].astype(jnp.float32)
+
+
+def depthwise_and_sums(tile, rims, weight, add, up, down, small, slides, tiles):
+    side, _, channels = tile.shape
+    rest, rows = up.shape[0], up.shape[1]
+    chunk = small.shape[1]
+    operands = [tile, *rims, weight, add]
+    fixed = lambda shape: pl.BlockSpec(
+        shape, lambda c: (0,) * len(shape), pipeline_mode=pl.Buffered(buffer_count=1)
+    )
+    shape = jax.ShapeDtypeStruct
+    wide, narrow = jnp.float32, jnp.bfloat16
+    return pl.pallas_call(
+        functools.partial(back_body, (slides, tiles)),
+        out_shape=(
+            shape(tile.shape, narrow),
+            shape((rows, channels), wide),
+            shape((rows, channels), wide),
+            shape(small.shape, wide),
+        ),
+        grid=(channels // lanes,),
+        in_specs=[tile_spec(o.shape) for o in operands]
+        + [fixed(up.shape), fixed(down.shape), fixed(small.shape)],
+        out_specs=(
+            tile_spec(tile.shape),
+            fixed((rows, channels)),
+            fixed((rows, channels)),
+            fixed(small.shape),
+        ),
+        scratch_shapes=[
+            pltpu.VMEM((side + 6, side + 16, lanes), wide),
+            pltpu.VMEM((side + 6, side, lanes), wide),
+            pltpu.VMEM((side, side, lanes), wide),
+            pltpu.VMEM((rest - 1, rows, channels), narrow),
+            pltpu.VMEM((rest - 1, rows, channels), narrow),
+            pltpu.VMEM((tiles - 1, chunk, channels), wide),
+            pltpu.VMEM((slides, chunk, channels), wide),
+            pltpu.VMEM((tiles, chunk, channels), wide),
+            pltpu.SemaphoreType.DMA((2, rest - 1)),
+            pltpu.SemaphoreType.DMA((2, rest - 1)),
+            pltpu.SemaphoreType.DMA((2, tiles - 1)),
+            pltpu.SemaphoreType.DMA((2, slides - 1)),
+            pltpu.SemaphoreType.DMA((2, tiles - 1)),
+        ],
+        compiler_params=params(collective_id=3, has_side_effects=True),
+        cost_estimate=pl.CostEstimate(
+            flops=2 * 10**10, bytes_accessed=8 << 20, transcendentals=0
+        ),
+        name="depthwise_and_sums",
+    )(*operands, up, down, small)
 
 
 def tile_spec(shape):
     return pl.BlockSpec(shape[:-1] + (lanes,), lambda c: (0,) * (len(shape) - 1) + (c,))
 
 
-def depthwise(tile, rims, weight, add=None):
+def depthwise(tile, rims, weight):
     side, _, channels = tile.shape
-    operands = [tile, *rims, weight] + ([] if add is None else [add])
-    out = jax.ShapeDtypeStruct(tile.shape, jnp.float32 if add is None else jnp.bfloat16)
+    operands = [tile, *rims, weight]
     flops = 2 * 49 * side * side * channels
     return pl.pallas_call(
-        functools.partial(conv_body, add is not None),
-        out_shape=out,
+        conv_body,
+        out_shape=jax.ShapeDtypeStruct(tile.shape, jnp.float32),
         grid=(channels // lanes,),
         in_specs=[tile_spec(o.shape) for o in operands],
-        out_specs=tile_spec(out.shape),
+        out_specs=tile_spec(tile.shape),
         scratch_shapes=[
             pltpu.VMEM((side + 6, side + 16, lanes), jnp.float32),
             pltpu.VMEM((side + 6, side, lanes), jnp.float32),
             pltpu.VMEM((side, side, lanes), jnp.float32),
         ],
         compiler_params=params(),
-        cost_estimate=pl.CostEstimate(flops=100 * flops, bytes_accessed=8 << 20, transcendentals=0),
+        cost_estimate=pl.CostEstimate(flops=260 * flops, bytes_accessed=8 << 20, transcendentals=0),
         name="depthwise",
     )(*operands)
 
@@ -238,7 +409,7 @@
             pltpu.VMEM((side, side, lanes), jnp.float32),
         ],
         compiler_params=params(),
-        cost_estimate=pl.CostEstimate(flops=100 * flops, bytes_accessed=8 << 20, transcendentals=0),
+        cost_estimate=pl.CostEstimate(flops=260 * flops, bytes_accessed=8 << 20, transcendentals=0),
         name="kernel_grad",
     )(*operands)
 
@@ -556,14 +727,6 @@
             total = total + came.astype(jnp.float32)
         return total if last else total.astype(jnp.bfloat16)
 
-    def everywhere(self, value):
-        for axis in self.names[::-1]:
-            step = 1
-            while step < self.sizes[axis]:
-                value = value + self.send(value, axis, lambda i, s=step: i ^ s)
-                step *= 2
-        return value
-
 
 def on_device(
     features,
@@ -606,25 +769,28 @@
         tiles,
     )
     conv_tile = conv_grad.reshape(side, side, channels)
-    grad_rims = exchange_rims(conv_tile, table, tiles, 1)
-
+    kernel_sum = kernel_grad(tile, rims, conv_tile)
     up_part = grid.scatter(up_grad, 1, "lo")
     down_part = grid.scatter(down_grad, 1, "hi")
-    up_part = grid.scatter(up_part, 0, "rest", last=True)
-    down_part = grid.scatter(down_part, 0, "rest", last=True)
+    conv_tile, kernel_sum, up_part, down_part = lax.optimization_barrier(
+        (conv_tile, kernel_sum, up_part, down_part)
+    )
+    small = jnp.concatenate([kernel_sum, sums, bias.reshape(-1, channels)], 0)
+    count = small.shape[0]
+    small = jnp.pad(small, ((0, -count % (8 * tiles)), (0, 0))).reshape(tiles, -1, channels)
+    grad_rims = exchange_rims(conv_tile, table, tiles, 1)
+    input_grad, up_part, down_part, small = depthwise_and_sums(
+        conv_tile, grad_rims, taps[::-1], grad, up_part, down_part, small, slides, tiles
+    )
+    small = small.reshape(-1, channels)
     weight_grads = jnp.concatenate([up_part, down_part], -1)[None]
-
-    kernel_sum = kernel_grad(tile, rims, conv_tile)
-    small = jnp.concatenate([kernel_sum, sums, bias.reshape(-1, channels)], 0)
-    small = grid.everywhere(small)
-    input_grad = depthwise(conv_tile, grad_rims, taps[::-1], grad)
     return (
         block_out.reshape(1, 1, side, side, channels),
         input_grad[None, None],
         weight_grads,
         small[:49].reshape(1, 7, 7, channels),
         small[49:53][None],
-        small[53:].reshape(1, hidden),
+        small[53:count].reshape(1, hidden),
     )
 
 

time: 210 us -> 185 us (0.88)
  waiting for transfers between devices: 32.7 us -> 0.01 us
  Pallas kernels: 146 us -> 160 us
  starting transfers between devices: 14.4 us -> 2.1 us
  local copies, waits for them, and re-layouts: 7.29 us -> 12.3 us
    ppermute x13 -> x2, waiting for transfers between devices: 32.7 us -> 0.01 us  [send(): return lax.ppermute(value, ('slide', 'tile'), self.perm(axis, move))]
    pallas_call x2, Pallas kernels: 33.4 us -> 55.5 us  [the longest x1 38.8 us: depthwise_and_sums(): pl.pallas_call(functools.partial(back_body, (slides, tiles)), out_shape=(...]
    ppermute x13 -> x2, starting transfers between devices: 14.4 us -> 2.1 us  [send(): return lax.ppermute(value, ('slide', 'tile'), self.perm(axis, move))]
    pallas_call x2, Pallas kernels: 33.8 us -> 26 us  [exchange_rims(): pl.pallas_call(functools.partial(rim_body, count), out_shape=(edge, edge,...]
    unnamed x17 -> x20, local copies, waits for them, and re-layouts: 2.39 us -> 5.18 us
    add x7 -> x0, other arithmetic: 2.12 us -> none  [the longest x5 1.97 us: everywhere(): value = value + self.send(value, axis, lambda i, s=step: i ^ s)]
  transfers between devices with their start and end apart: 13 -> 2, of which waited for: 6 -> 0; matrix products, arithmetic and copies ran while one was open for 4% -> 3% of each run, Pallas kernels for 17% -> 9%
where the time goes in v3:
time: 185 us; the launch traced here: 184 us
  Pallas kernels  160 us (86%)
  local copies, waits for them, and re-layouts  12.3 us (7%)
  other arithmetic  7.95 us (4%)
  starting transfers between devices  2.1 us (1%)
    pallas_call x1, Pallas kernels, mlp(): pl.pallas_call(functools.partial(mlp_body, (rest, his, los)), out_shape=(...  61.9 us
    pallas_call x1, Pallas kernels, depthwise_and_sums(): pl.pallas_call(functools.partial(back_body, (slides, tiles)), out_shape=(...  38.8 us
    pallas_call x2, Pallas kernels, exchange_rims(): pl.pallas_call(functools.partial(rim_body, count), out_shape=(edge, edge,...  26 us
    pallas_call x1, Pallas kernels, depthwise(): pl.pallas_call(conv_body, out_shape=jax.ShapeDtypeStruct(tile.shape, jnp....  16.7 us
    pallas_call x1, Pallas kernels, kernel_grad(): pl.pallas_call(kernel_grad_body, out_shape=jax.ShapeDtypeStruct((49, chan...  16.4 us
    unnamed x20, local copies, waits for them, and re-layouts  5.18 us
    convert_element_type x2, other arithmetic, scatter(): return total if last else total.astype(jnp.bfloat16)  4.03 us
  transfers between devices with their start and end apart: 2, of which 0 were waited for; matrix products, arithmetic and copies ran while one was open for 3% of the time, Pallas kernels for 9%

profile of v3, /device:TPU:0, one launch (start us, length us, event | category | flops | bytes accessed | tf_op | source)
XLA Modules:
  0.0 183.6 jit_solution(7448274817093675945)
XLA Ops:
  0.6 1.3 reduce
  1.9 0.7 reshape_squeeze.9.weight_ref
  3.3 14.3 %rims0.1 = (f32[3,48,768]{2,1,0:T(8,128)}, f32[3,48,768]{2,1,0:T(8,128)}, f32[32,8,768]{2,1,0:T(8,128)}, f32[32,8,768]{2,1,0:T(8,128)}) custom-call(s32[4,8]{1,0:T(4,128)} %bitcast.48, bf16[32,32,768]{2,1,0:T(8,128)(2,1)} %bitcast.41), custom_call_target="tpu_custom_call" | custom-call | flops 10000000000 | bytes 8388608 | tf_op jit(solution)/shard_map/rims0/pallas_call | solution.py:92
  17.6 16.7 %depthwise.1 = f32[32,32,768]{2,1,0:T(8,128)} custom-call(bf16[32,32,768]{2,1,0:T(8,128)(2,1)} %bitcast.42, f32[3,48,768]{2,1,0:T(8,128)} %get-tuple-element.28.top, f32[3,48,768]{2,1,0:T(8,128)} %get-tuple-element.29.bottom, f32[32,8,768]{2,1,0:T(8,128)} %get-tuple-element.30.west, f32[32,8,768]{2,1,0:T(8,128)} %get-tuple-element.31.east, ...), custom_call_target="tpu_custom_call" | custom-call | flops 20038287360 | bytes 8388608 | tf_op jit(solution)/shard_map/depthwise/pallas_call | solution.py:344
  34.3 0.5 broadcast_in_dim.12.keep_ref
  34.8 61.9 %mlp.1 = (bf16[1024,768]{1,0:T(8,128)(2,1)}, bf16[1024,768]{1,0:T(8,128)(2,1)}, bf16[4,2,96,768]{3,2,1,0:T(8,128)(2,1)}, bf16[4,2,96,768]{3,2,1,0:T(8,128)(2,1)}...) custom-call(f32[1024,768]{1,0:T(8,128)} %bitcast.50, bf16[1024,768]{1,0:T(8,128)(2,1)} %bitcast.43, bf16[1024,768]{1,0:T(8,128)(2,1)} %bitcast.45, ...), custom_call_target="tpu_custom_call" | custom-call | flops 28991029248 | bytes 33554432 | tf_op jit(solution)/shard_map/mlp/pallas_call | solution.py:631
  96.8 0.0 copy-start.2
  96.8 1.2 dynamic-slice_bitcast_fusion.1
  98.0 1.5 collective-permute-start
  99.5 0.0 copy-done.2
  99.5 0.9 dynamic-slice_bitcast_fusion
  100.4 0.6 collective-permute-start.1
  100.9 0.0 copy-start.4
  100.9 0.0 copy-start.7
  100.9 0.0 copy-start.3
  100.9 16.4 %kernel_grad.1 = f32[49,768]{1,0:T(8,128)} custom-call(bf16[32,32,768]{2,1,0:T(8,128)(2,1)} %bitcast.44, f32[3,48,768]{2,1,0:T(8,128)} %get-tuple-element.28.top, f32[3,48,768]{2,1,0:T(8,128)} %get-tuple-element.29.bottom, f32[32,8,768]{2,1,0:T(8,128)} %get-tuple-element.30.west, f32[32,8,768]{2,1,0:T(8,128)} %get-tuple-element.31.east, ...), custom_call_target="tpu_custom_call" | custom-call | flops 20038287360 | bytes 8388608 | tf_op jit(solution)/shard_map/kernel_grad/pallas_call | solution.py:400
  117.3 0.0 copy-done.4
  117.3 2.0 %rev.3.weight_ref = f32[49,768]{1,0:T(8,128)} reverse(f32[49,768]{1,0:T(8,128)S(1)} %copy-done.4), dimensions={0} | reverse | bytes 301056 | tf_op jit(solution)/shard_map/rev | solution.py:783
  119.3 0.0 copy-done.7
  119.3 0.0 collective-permute-done
  119.3 0.0 copy-done.3
  119.3 2.0 %fusion.1.up = bf16[4,96,768]{2,1,0:T(8,128)(2,1)} fusion(bf16[4,96,768]{2,1,0:T(8,128)(2,1)} %collective-permute-done, s32[]{:T(128)S(6)} %select_n.18, bf16[4,2,96,768]{3,2,1,0:T(8,128)(2,1)S(1)} %copy-done.3), kind=kLoop, calls=%fused_computation.3 | loop fusion | flops 1179648 | bytes 1769476 | tf_op jit(solution)/shard_map/convert_element_type | solution.py:728
  121.4 0.0 collective-permute-done.1
  121.4 2.0 %fusion.down = bf16[4,96,768]{2,1,0:T(8,128)(2,1)} fusion(bf16[4,96,768]{2,1,0:T(8,128)(2,1)} %collective-permute-done.1, s32[]{:T(128)S(6)} %select_n.21, bf16[4,2,96,768]{3,2,1,0:T(8,128)(2,1)S(1)} %copy-done.2), kind=kLoop, calls=%fused_computation.1 | loop fusion | flops 1179648 | bytes 1769476 | tf_op jit(solution)/shard_map/convert_element_type | solution.py:728
  123.4 0.0 copy-start.5
  123.4 0.0 copy-start.6
  123.4 11.7 %rims1.1 = (f32[3,48,768]{2,1,0:T(8,128)}, f32[3,48,768]{2,1,0:T(8,128)}, f32[32,8,768]{2,1,0:T(8,128)}, f32[32,8,768]{2,1,0:T(8,128)}) custom-call(s32[4,8]{1,0:T(4,128)} %bitcast.49, bf16[32,32,768]{2,1,0:T(8,128)(2,1)} %bitcast.52), custom_call_target="tpu_custom_call" | custom-call | flops 10000000000 | bytes 8388608 | tf_op jit(solution)/shard_map/rims1/pallas_call | solution.py:92
  135.1 0.0 copy-done.5
  135.1 0.0 copy-done.6
  135.1 0.7 select_maximum_fusion
  135.8 38.8 %depthwise_and_sums.1 = (bf16[32,32,768]{2,1,0:T(8,128)(2,1)}, f32[96,768]{1,0:T(8,128)}, f32[96,768]{1,0:T(8,128)}, f32[4,16,768]{2,1,0:T(8,128)}) custom-call(bf16[32,32,768]{2,1,0:T(8,128)(2,1)} %bitcast.53, f32[3,48,768]{2,1,0:T(8,128)} %get-tuple-element.37.top, f32[3,48,768]{2,1,0:T(8,128)} %get-tuple-element.38.bottom, ...), custom_call_target="tpu_custom_call" | custom-call | flops 20000000000 | bytes 8388608 | tf_op jit(solution)/shard_map/depthwise_and_sums/pallas_call | solution.py:296
  174.6 0.0 copy-start
  174.6 1.0 slice.12
  175.7 1.4 slice_bitcast_fusion
  177.1 0.8 reshape.53
  177.9 0.6 copy.21
  178.5 1.9 %maximum_bitcast_fusion = f32[1,96,1536]{2,1,0:T(8,128)} fusion(f32[96,768]{1,0:T(8,128)} %get-tuple-element.48, f32[96,768]{1,0:T(8,128)} %get-tuple-element.47), kind=kLoop, calls=%fused_computation.4 | loop fusion | flops 147456 | bytes 1179648 | tf_op jit(solution)/shard_map/broadcast_in_dim | solution.py:786
  180.5 0.0 copy-done
  180.5 0.0 copy-start.1
  180.5 1.1 copy.29
  181.6 0.8 copy-done.1
  182.4 1.1 copy.30
  (2 shorter events, 0.0 us)
Async XLA Ops:
  96.8 2.7 %copy-start.2 = (bf16[4,2,96,768]{3,2,1,0:T(8,128)(2,1)S(1)}, bf16[4,2,96,768]{3,2,1,0:T(8,128)(2,1)}, u32[]{:S(2)}) copy-start(bf16[4,2,96,768]{3,2,1,0:T(8,128)(2,1)} %get-tuple-element.35) | copy-start | bytes 3538948
  98.0 21.3 %collective-permute-start = (bf16[4,96,768]{2,1,0:T(8,128)(2,1)S(1)}, bf16[4,96,768]{2,1,0:T(8,128)(2,1)}, u32[]{:S(2)}, u32[]{:S(2)}) collective-permute-start(bf16[4,96,768]{2,1,0:T(8,128)(2,1)S(1)} %dynamic-slice_bitcast_fusion.1), channel_id=1, source_target_pairs={{0,1},{1,0},{2,3},{3,2},{4,5},{5,4},{6,7},{7,6},{8,9},{9,8},{10,11... | collective-permute-start | bytes 1769480 | tf_op jit(solution)/shard_map/ppermute | solution.py:718
  100.4 21.0 %collective-permute-start.1 = (bf16[4,96,768]{2,1,0:T(8,128)(2,1)}, bf16[4,96,768]{2,1,0:T(8,128)(2,1)}, u32[]{:S(2)}, u32[]{:S(2)}) collective-permute-start(bf16[4,96,768]{2,1,0:T(8,128)(2,1)} %dynamic-slice_bitcast_fusion), channel_id=1, source_target_pairs={{0,2},{1,3},{2,0},{3,1},{4,6},{5,7},{6,4},{7,5},{8,10},{9,11},{10,... | collective-permute-start | bytes 1769480 | tf_op jit(solution)/shard_map/ppermute | solution.py:718
  100.9 16.4 %copy-start.4 = (f32[49,768]{1,0:T(8,128)S(1)}, f32[49,768]{1,0:T(8,128)}, u32[]{:S(2)}) copy-start(f32[49,768]{1,0:T(8,128)} %reshape_squeeze.9.weight_ref) | copy-start | bytes 451588
  100.9 18.3 %copy-start.7 = (f32[8,1,384]{2,1,0:T(1,128)S(1)}, f32[8,1,384]{2,1,0:T(1,128)}, u32[]{:S(2)}) copy-start(f32[8,1,384]{2,1,0:T(1,128)} %get-tuple-element.45) | copy-start | bytes 36868
  100.9 18.4 %copy-start.3 = (bf16[4,2,96,768]{3,2,1,0:T(8,128)(2,1)S(1)}, bf16[4,2,96,768]{3,2,1,0:T(8,128)(2,1)}, u32[]{:S(2)}) copy-start(bf16[4,2,96,768]{3,2,1,0:T(8,128)(2,1)} %get-tuple-element.34) | copy-start | bytes 3538948
  123.4 11.7 %copy-start.5 = (f32[49,768]{1,0:T(8,128)S(1)}, f32[49,768]{1,0:T(8,128)}, u32[]{:S(2)}) copy-start(f32[49,768]{1,0:T(8,128)} %kernel_grad.1) | copy-start | bytes 451588
  123.4 11.7 %copy-start.6 = (f32[4,768]{1,0:T(4,128)S(1)}, f32[4,768]{1,0:T(4,128)}, u32[]{:S(2)}) copy-start(f32[4,768]{1,0:T(4,128)} %get-tuple-element.44) | copy-start | bytes 36868
  174.6 5.8 %copy-start = (bf16[1024,768]{1,0:T(8,128)(2,1)S(1)}, bf16[1024,768]{1,0:T(8,128)(2,1)}, u32[]{:S(2)}) copy-start(bf16[1024,768]{1,0:T(8,128)(2,1)} %get-tuple-element.32) | copy-start | bytes 4718596
  180.5 2.0 %copy-start.1 = (bf16[32,32,768]{2,1,0:T(8,128)(2,1)S(1)}, bf16[32,32,768]{2,1,0:T(8,128)(2,1)}, u32[]{:S(2)}) copy-start(bf16[32,32,768]{2,1,0:T(8,128)(2,1)} %get-tuple-element.46) | copy-start | bytes 4718596

commit v4 on v3

--- a/solution.py
+++ b/solution.py
@@ -20,9 +20,15 @@
     return pltpu.CompilerParams(vmem_limit_bytes=vmem_bytes, **more)
 
 
-def rim_body(
-    count, table, tile, top, bottom, west, east, strips, sends, slots, send_sem, recv_sem
-):
+def rim_body(count, rest, table, tile, *refs):
+    if rest:
+        part, top, bottom, west, east, part_out, *refs = refs
+        strips, sends, slots, send_sem, recv_sem, part_recv, part_sems = refs
+    else:
+        top, bottom, west, east, strips, sends, slots, send_sem, recv_sem = refs
+    slide = lax.axis_index("slide")
+    far, core = slide // 2, lax.rem(slide, 2)
+    next_far = [lax.rem(far + o, rest) for o in range(1, rest)]
     side = tile.shape[0]
     me = lax.axis_index("tile")
     peers = [lax.rem(me + offset, count) for offset in range(1, count)]
@@ -30,6 +36,11 @@
     for peer in peers:
         pl.semaphore_signal(
             barrier, inc=1, device_id={"tile": peer}, device_id_type=pl.DeviceIdType.MESH
+        )
+    for at in next_far:
+        device = {"slide": at * 2 + core}
+        pl.semaphore_signal(
+            barrier, inc=1, device_id=device, device_id_type=pl.DeviceIdType.MESH
         )
     for k in range(3):
         at = pl.ds(k * side, side)
@@ -40,7 +51,19 @@
         strips[2, 3 * h : 3 * h + 3] = row[side - 3 :]
         strips[3, 3 * h : 3 * h + 3] = row[:3]
     slots[0] = jnp.zeros(slots.shape[1:], slots.dtype)
-    pl.semaphore_wait(barrier, count - 1)
+    pl.semaphore_wait(barrier, count - 1 + len(next_far))
+    far_copies = []
+    for i, at in enumerate(next_far):
+        copy = pltpu.make_async_remote_copy(
+            src_ref=part.at[at],
+            dst_ref=part_recv.at[i],
+            send_sem=part_sems.at[0, i],
+            recv_sem=part_sems.at[1, i],
+            device_id={"slide": at * 2 + core},
+            device_id_type=pl.DeviceIdType.MESH,
+        )
+        copy.start()
+        far_copies.append(copy)
     copies = []
     for i, peer in enumerate(peers):
         kind = jnp.int32(0)
@@ -82,31 +105,46 @@
     for h in range(side):
         west[h, 5:8] = strips[0, 3 * h : 3 * h + 3]
         east[h, 0:3] = strips[1, 3 * h : 3 * h + 3]
-
-
-def exchange_rims(tile, table, count, call):
+    if rest:
+        part_out[...] = part[far].astype(jnp.float32)
+        for i, copy in enumerate(far_copies):
+            copy.wait()
+            part_out[...] += part_recv[i].astype(jnp.float32)
+
+
+def exchange_rims(tile, table, count, call, part=None):
     side, _, channels = tile.shape
     vmem = pl.BlockSpec(memory_space=pltpu.VMEM)
     edge = jax.ShapeDtypeStruct((3, side + 16, channels), jnp.float32)
     flank = jax.ShapeDtypeStruct((side, 8, channels), jnp.float32)
+    rest, outs, more, operands = 0, (edge, edge, flank, flank), [], [table, tile]
+    if part is not None:
+        rest = part.shape[0]
+        outs += (jax.ShapeDtypeStruct(part.shape[1:], jnp.float32),)
+        more = [
+            pltpu.VMEM((rest - 1,) + part.shape[1:], part.dtype),
+            pltpu.SemaphoreType.DMA((2, rest - 1)),
+        ]
+        operands.append(part)
     return pl.pallas_call(
-        functools.partial(rim_body, count),
-        out_shape=(edge, edge, flank, flank),
-        in_specs=[pl.BlockSpec(memory_space=pltpu.SMEM), vmem],
-        out_specs=(vmem,) * 4,
+        functools.partial(rim_body, count, rest),
+        out_shape=outs,
+        in_specs=[pl.BlockSpec(memory_space=pltpu.SMEM)] + [vmem] * (len(operands) - 1),
+        out_specs=(vmem,) * len(outs),
         scratch_shapes=[
             pltpu.VMEM((4, 3 * side, channels), jnp.float32),
             pltpu.VMEM((count - 1, 3 * side, channels), jnp.bfloat16),
             pltpu.VMEM((count, 3 * side, channels), jnp.bfloat16),
             pltpu.SemaphoreType.DMA((count - 1,)),
             pltpu.SemaphoreType.DMA((count - 1,)),
+            *more,
         ],
         compiler_params=params(collective_id=call, has_side_effects=True),
         cost_estimate=pl.CostEstimate(
             flops=10**10, bytes_accessed=8 << 20, transcendentals=0
         ),
         name="rims" + str(call),
-    )(table, tile)
+    )(*operands)
 
 
 def fill(ext, tile_ref, top_ref, bottom_ref, west_ref, east_ref):
@@ -123,7 +161,9 @@
     out_ref[...] = total[...]
 
 
-def conv_sum(tile_ref, top, bottom, west, east, weight_ref, ext, shifted, total):
+def conv_sum(
+    tile_ref, top, bottom, west, east, weight_ref, ext, shifted, total, flipped=False
+):
     side = tile_ref.shape[0]
     fill(ext, tile_ref, top, bottom, west, east)
     for b in range(7):
@@ -132,9 +172,8 @@
         else:
             shifted[...] = ext[:, 5 + b : 5 + b + side]
             source, base = shifted, 0
-        taps = [
-            jnp.broadcast_to(weight_ref[a * 7 + b : a * 7 + b + 1, :], (8, lanes)) for a in range(7)
-        ]
+        spots = [48 - a * 7 - b if flipped else a * 7 + b for a in range(7)]
+        taps = [jnp.broadcast_to(weight_ref[at : at + 1, :], (8, lanes)) for at in spots]
 
         def rows(step, carry, b=b, source=source, base=base, taps=taps):
             first = step * row_step
@@ -167,22 +206,18 @@
     east,
     weight_ref,
     add_ref,
-    up,
     down,
     small,
     out_ref,
-    up_out,
     down_out,
     small_out,
     ext,
     shifted,
     total,
-    up_recv,
     down_recv,
     small_recv,
     slide_slots,
     tile_slots,
-    up_sems,
     down_sems,
     small_sems,
     slide_sems,
@@ -240,7 +275,7 @@
                 barrier, inc=1, device_id=peer, device_id_type=pl.DeviceIdType.MESH
             )
         pl.semaphore_wait(barrier, len(peers))
-        for copy in small_copies() + far_copies(up, up_recv, up_sems):
+        for copy in small_copies():
             copy.start()
 
     @pl.when(step == 1)
@@ -264,7 +299,7 @@
         for copy in tile_copies():
             copy.start()
 
-    conv_sum(tile_ref, top, bottom, west, east, weight_ref, ext, shifted, total)
+    conv_sum(tile_ref, top, bottom, west, east, weight_ref, ext, shifted, total, True)
     out_ref[...] = (add_ref[...].astype(jnp.float32) + total[...]).astype(jnp.bfloat16)
 
     @pl.when(step == pl.num_programs(0) - 1)
@@ -273,19 +308,15 @@
             copy.wait()
         for i in range(tiles):
             small_out[i] = tile_slots[lax.rem(tile - i + tiles, tiles)]
-        for part, recv, sems, out in (
-            (up, up_recv, up_sems, up_out),
-            (down, down_recv, down_sems, down_out),
-        ):
-            out[...] = part[far].astype(jnp.float32)
-            for i, copy in enumerate(far_copies(part, recv, sems)):
-                copy.wait()
-                out[...] += recv[i].astype(jnp.float32)
-
-
-def depthwise_and_sums(tile, rims, weight, add, up, down, small, slides, tiles):
+        down_out[...] = down[far].astype(jnp.float32)
+        for i, copy in enumerate(far_copies(down, down_recv, down_sems)):
+            copy.wait()
+            down_out[...] += down_recv[i].astype(jnp.float32)
+
+
+def depthwise_and_sums(tile, rims, weight, add, down, small, slides, tiles):
     side, _, channels = tile.shape
-    rest, rows = up.shape[0], up.shape[1]
+    rest, rows = down.shape[0], down.shape[1]
     chunk = small.shape[1]
     operands = [tile, *rims, weight, add]
     fixed = lambda shape: pl.BlockSpec(
@@ -298,15 +329,13 @@
         out_shape=(
             shape(tile.shape, narrow),
             shape((rows, channels), wide),
-            shape((rows, channels), wide),
             shape(small.shape, wide),
         ),
         grid=(channels // lanes,),
         in_specs=[tile_spec(o.shape) for o in operands]
-        + [fixed(up.shape), fixed(down.shape), fixed(small.shape)],
+        + [fixed(down.shape), fixed(small.shape)],
         out_specs=(
             tile_spec(tile.shape),
-            fixed((rows, channels)),
             fixed((rows, channels)),
             fixed(small.shape),
         ),
@@ -315,11 +344,9 @@
             pltpu.VMEM((side + 6, side, lanes), wide),
             pltpu.VMEM((side, side, lanes), wide),
             pltpu.VMEM((rest - 1, rows, channels), narrow),
-            pltpu.VMEM((rest - 1, rows, channels), narrow),
             pltpu.VMEM((tiles - 1, chunk, channels), wide),
             pltpu.VMEM((slides, chunk, channels), wide),
             pltpu.VMEM((tiles, chunk, channels), wide),
-            pltpu.SemaphoreType.DMA((2, rest - 1)),
             pltpu.SemaphoreType.DMA((2, rest - 1)),
             pltpu.SemaphoreType.DMA((2, tiles - 1)),
             pltpu.SemaphoreType.DMA((2, slides - 1)),
@@ -330,7 +357,7 @@
             flops=2 * 10**10, bytes_accessed=8 << 20, transcendentals=0
         ),
         name="depthwise_and_sums",
-    )(*operands, up, down, small)
+    )(*operands, down, small)
 
 
 def tile_spec(shape):
@@ -778,9 +805,9 @@
     small = jnp.concatenate([kernel_sum, sums, bias.reshape(-1, channels)], 0)
     count = small.shape[0]
     small = jnp.pad(small, ((0, -count % (8 * tiles)), (0, 0))).reshape(tiles, -1, channels)
-    grad_rims = exchange_rims(conv_tile, table, tiles, 1)
-    input_grad, up_part, down_part, small = depthwise_and_sums(
-        conv_tile, grad_rims, taps[::-1], grad, up_part, down_part, small, slides, tiles
+    *grad_rims, up_part = exchange_rims(conv_tile, table, tiles, 1, up_part)
+    input_grad, down_part, small = depthwise_and_sums(
+        conv_tile, grad_rims, taps, grad, down_part, small, slides, tiles
     )
     small = small.reshape(-1, channels)
     weight_grads = jnp.concatenate([up_part, down_part], -1)[None]

time: 185 us -> 181 us (0.978)
  Pallas kernels: 160 us -> 157 us
  local copies, waits for them, and re-layouts: 12.3 us -> 10.2 us
    pallas_call x1, Pallas kernels: 38.8 us -> 30.1 us  [depthwise_and_sums(): pl.pallas_call(functools.partial(back_body, (slides, tiles)), out_shape=(...]
    pallas_call x2, Pallas kernels: 26 us -> 31.7 us  [exchange_rims(): pl.pallas_call(functools.partial(rim_body, count, rest), out_shape=outs,...]
    rev x1 -> x0, local copies, waits for them, and re-layouts: 1.96 us -> none  [on_device(): taps[::-1]]
  transfers between devices with their start and end apart: 2 -> 2, of which waited for: 0 -> 0; matrix products, arithmetic and copies ran while one was open for 3% -> 2% of each run, Pallas kernels for 9% -> 9%
where the time goes in v4:
time: 181 us; the launch traced here: 179 us
  Pallas kernels  157 us (87%)
  local copies, waits for them, and re-layouts  10.2 us (6%)
  other arithmetic  8.46 us (5%)
  starting transfers between devices  2.16 us (1%)
    pallas_call x1, Pallas kernels, mlp(): pl.pallas_call(functools.partial(mlp_body, (rest, his, los)), out_shape=(...  61.9 us
    pallas_call x2, Pallas kernels, exchange_rims(): pl.pallas_call(functools.partial(rim_body, count, rest), out_shape=outs,...  31.7 us
    pallas_call x1, Pallas kernels, depthwise_and_sums(): pl.pallas_call(functools.partial(back_body, (slides, tiles)), out_shape=(...  30.1 us
    pallas_call x1, Pallas kernels, depthwise(): pl.pallas_call(conv_body, out_shape=jax.ShapeDtypeStruct(tile.shape, jnp....  16.7 us
    pallas_call x1, Pallas kernels, kernel_grad(): pl.pallas_call(kernel_grad_body, out_shape=jax.ShapeDtypeStruct((49, chan...  16.4 us
    unnamed x20, local copies, waits for them, and re-layouts  5.18 us
    convert_element_type x2, other arithmetic, scatter(): return total if last else total.astype(jnp.bfloat16)  4.03 us
  transfers between devices with their start and end apart: 2, of which 0 were waited for; matrix products, arithmetic and copies ran while one was open for 2% of the time, Pallas kernels for 9%

profile of v4, /device:TPU:0, one launch (start us, length us, event | category | flops | bytes accessed | tf_op | source)
XLA Modules:
  0.0 179.0 jit_solution(4003659059193392429)
XLA Ops:
  0.6 1.3 reduce
  1.9 0.7 reshape_squeeze.9.weight_ref
  3.3 14.3 %rims0.1 = (f32[3,48,768]{2,1,0:T(8,128)}, f32[3,48,768]{2,1,0:T(8,128)}, f32[32,8,768]{2,1,0:T(8,128)}, f32[32,8,768]{2,1,0:T(8,128)}) custom-call(s32[4,8]{1,0:T(4,128)} %bitcast.48, bf16[32,32,768]{2,1,0:T(8,128)(2,1)} %bitcast.41), custom_call_target="tpu_custom_call" | custom-call | flops 10000000000 | bytes 8388608 | tf_op jit(solution)/shard_map/rims0/pallas_call | solution.py:129
  17.6 16.7 %depthwise.1 = f32[32,32,768]{2,1,0:T(8,128)} custom-call(bf16[32,32,768]{2,1,0:T(8,128)(2,1)} %bitcast.42, f32[3,48,768]{2,1,0:T(8,128)} %get-tuple-element.28.top, f32[3,48,768]{2,1,0:T(8,128)} %get-tuple-element.29.bottom, f32[32,8,768]{2,1,0:T(8,128)} %get-tuple-element.30.west, f32[32,8,768]{2,1,0:T(8,128)} %get-tuple-element.31.east, ...), custom_call_target="tpu_custom_call" | custom-call | flops 20038287360 | bytes 8388608 | tf_op jit(solution)/shard_map/depthwise/pallas_call | solution.py:371
  34.3 0.5 broadcast_in_dim.12.keep_ref
  34.8 61.9 %mlp.1 = (bf16[1024,768]{1,0:T(8,128)(2,1)}, bf16[1024,768]{1,0:T(8,128)(2,1)}, bf16[4,2,96,768]{3,2,1,0:T(8,128)(2,1)}, bf16[4,2,96,768]{3,2,1,0:T(8,128)(2,1)}...) custom-call(f32[1024,768]{1,0:T(8,128)} %bitcast.50, bf16[1024,768]{1,0:T(8,128)(2,1)} %bitcast.43, bf16[1024,768]{1,0:T(8,128)(2,1)} %bitcast.45, ...), custom_call_target="tpu_custom_call" | custom-call | flops 28991029248 | bytes 33554432 | tf_op jit(solution)/shard_map/mlp/pallas_call | solution.py:658
  96.8 0.0 copy-start.2
  96.8 1.2 dynamic-slice_bitcast_fusion.1
  98.0 1.5 collective-permute-start
  99.5 0.0 copy-done.2
  99.5 0.6 collective-permute-start.1
  100.2 0.0 copy-start.7
  100.2 0.0 copy-start.3
  100.2 16.4 %kernel_grad.1 = f32[49,768]{1,0:T(8,128)} custom-call(bf16[32,32,768]{2,1,0:T(8,128)(2,1)} %bitcast.44, f32[3,48,768]{2,1,0:T(8,128)} %get-tuple-element.28.top, f32[3,48,768]{2,1,0:T(8,128)} %get-tuple-element.29.bottom, f32[32,8,768]{2,1,0:T(8,128)} %get-tuple-element.30.west, f32[32,8,768]{2,1,0:T(8,128)} %get-tuple-element.31.east, ...), custom_call_target="tpu_custom_call" | custom-call | flops 20038287360 | bytes 8388608 | tf_op jit(solution)/shard_map/kernel_grad/pallas_call | solution.py:427
  116.6 0.0 copy-done.7
  116.6 0.6 reduce.1
  117.2 0.7 reshape.50
  117.9 0.0 collective-permute-done
  117.9 0.0 copy-done.3
  117.9 2.0 %fusion.1.refs_0_ = bf16[4,96,768]{2,1,0:T(8,128)(2,1)} fusion(bf16[4,96,768]{2,1,0:T(8,128)(2,1)} %collective-permute-done, s32[]{:T(128)S(6)} %select_n.18, bf16[4,2,96,768]{3,2,1,0:T(8,128)(2,1)S(1)} %copy-done.3), kind=kLoop, calls=%fused_computation.3 | loop fusion | flops 1179648 | bytes 1769476 | tf_op jit(solution)/shard_map/convert_element_type | solution.py:755
  119.9 0.0 collective-permute-done.1
  119.9 2.0 %fusion.down = bf16[4,96,768]{2,1,0:T(8,128)(2,1)} fusion(bf16[4,96,768]{2,1,0:T(8,128)(2,1)} %collective-permute-done.1, s32[]{:T(128)S(6)} %select_n.21, bf16[4,2,96,768]{3,2,1,0:T(8,128)(2,1)S(1)} %copy-done.2), kind=kLoop, calls=%fused_computation.1 | loop fusion | flops 1179648 | bytes 1769476 | tf_op jit(solution)/shard_map/convert_element_type | solution.py:755
  122.0 0.0 copy-start.5
  122.0 0.0 copy-start.6
  122.0 17.4 %rims1.1 = (f32[3,48,768]{2,1,0:T(8,128)}, f32[3,48,768]{2,1,0:T(8,128)}, f32[32,8,768]{2,1,0:T(8,128)}, f32[32,8,768]{2,1,0:T(8,128)}, f32[96,768]{1,0:T(8,128)}) custom-call(s32[4,8]{1,0:T(4,128)} %bitcast.49, bf16[32,32,768]{2,1,0:T(8,128)(2,1)} %bitcast.52, bf16[4,96,768]{2,1,0:T(8,128)(2,1)} %fusion.1.refs_0_), custom_call_target="tpu_custom_call" | custom-call | flops 10000000000 | bytes 8388608 | tf_op jit(solution)/shard_map/rims1/pallas_call | solution.py:129
  139.4 0.0 copy-done.5
  139.4 0.0 copy-done.6
  139.4 0.7 select_maximum_fusion
  140.1 0.0 copy-start.4
  140.1 30.1 %depthwise_and_sums.1 = (bf16[32,32,768]{2,1,0:T(8,128)(2,1)}, f32[96,768]{1,0:T(8,128)}, f32[4,16,768]{2,1,0:T(8,128)}) custom-call(bf16[32,32,768]{2,1,0:T(8,128)(2,1)} %bitcast.53, f32[3,48,768]{2,1,0:T(8,128)} %get-tuple-element.38.top, f32[3,48,768]{2,1,0:T(8,128)} %get-tuple-element.39.bottom, f32[32,8,768]{2,1,0:T(8,128)} %get-tuple-element.40.west, ...), custom_call_target="tpu_custom_call" | custom-call | flops 20000000000 | bytes 8388608 | tf_op jit(solution)/shard_map/depthwise_and_sums/pallas_call | solution.py:327
  170.2 0.0 copy-start
  170.2 1.0 slice.12
  171.2 1.4 slice_bitcast_fusion
  172.6 0.8 reshape.53
  173.4 0.6 copy.21
  174.1 0.0 copy-done.4
  174.1 1.8 %maximum_bitcast_fusion = f32[1,96,1536]{2,1,0:T(8,128)} fusion(f32[96,768]{1,0:T(8,128)} %get-tuple-element.48, f32[96,768]{1,0:T(8,128)S(1)} %copy-done.4), kind=kLoop, calls=%fused_computation.4 | loop fusion | flops 147456 | bytes 1179648 | tf_op jit(solution)/shard_map/broadcast_in_dim | solution.py:813
  175.9 0.0 copy-done
  175.9 0.0 copy-start.1
  175.9 1.1 copy.29
  177.0 0.8 copy-done.1
  177.9 1.1 copy.30
  (1 shorter events, 0.0 us)
Async XLA Ops:
  96.8 2.7 %copy-start.2 = (bf16[4,2,96,768]{3,2,1,0:T(8,128)(2,1)S(1)}, bf16[4,2,96,768]{3,2,1,0:T(8,128)(2,1)}, u32[]{:S(2)}) copy-start(bf16[4,2,96,768]{3,2,1,0:T(8,128)(2,1)} %get-tuple-element.35) | copy-start | bytes 3538948
  98.0 19.9 %collective-permute-start = (bf16[4,96,768]{2,1,0:T(8,128)(2,1)S(1)}, bf16[4,96,768]{2,1,0:T(8,128)(2,1)}, u32[]{:S(2)}, u32[]{:S(2)}) collective-permute-start(bf16[4,96,768]{2,1,0:T(8,128)(2,1)S(1)} %dynamic-slice_bitcast_fusion.1), channel_id=1, source_target_pairs={{0,1},{1,0},{2,3},{3,2},{4,5},{5,4},{6,7},{7,6},{8,9},{9,8},{10,11... | collective-permute-start | bytes 1769480 | tf_op jit(solution)/shard_map/ppermute | solution.py:745
  99.5 20.4 %collective-permute-start.1 = (bf16[4,96,768]{2,1,0:T(8,128)(2,1)S(1)}, bf16[4,96,768]{2,1,0:T(8,128)(2,1)}, u32[]{:S(2)}, u32[]{:S(2)}) collective-permute-start(bf16[4,96,768]{2,1,0:T(8,128)(2,1)S(1)} %dynamic-slice_bitcast_fusion), channel_id=1, source_target_pairs={{0,2},{1,3},{2,0},{3,1},{4,6},{5,7},{6,4},{7,5},{8,10},{9,11},{10,... | collective-permute-start | bytes 1769480 | tf_op jit(solution)/shard_map/ppermute | solution.py:745
  100.2 16.4 %copy-start.7 = (f32[8,1,384]{2,1,0:T(1,128)S(1)}, f32[8,1,384]{2,1,0:T(1,128)}, u32[]{:S(2)}) copy-start(f32[8,1,384]{2,1,0:T(1,128)} %get-tuple-element.45) | copy-start | bytes 36868
  100.2 17.7 %copy-start.3 = (bf16[4,2,96,768]{3,2,1,0:T(8,128)(2,1)S(1)}, bf16[4,2,96,768]{3,2,1,0:T(8,128)(2,1)}, u32[]{:S(2)}) copy-start(bf16[4,2,96,768]{3,2,1,0:T(8,128)(2,1)} %get-tuple-element.34) | copy-start | bytes 3538948
  122.0 17.4 %copy-start.5 = (f32[49,768]{1,0:T(8,128)S(1)}, f32[49,768]{1,0:T(8,128)}, u32[]{:S(2)}) copy-start(f32[49,768]{1,0:T(8,128)} %kernel_grad.1) | copy-start | bytes 451588
  122.0 17.4 %copy-start.6 = (f32[4,768]{1,0:T(4,128)S(1)}, f32[4,768]{1,0:T(4,128)}, u32[]{:S(2)}) copy-start(f32[4,768]{1,0:T(4,128)} %get-tuple-element.44) | copy-start | bytes 36868
  140.1 34.0 %copy-start.4 = (f32[96,768]{1,0:T(8,128)S(1)}, f32[96,768]{1,0:T(8,128)}, u32[]{:S(2)}) copy-start(f32[96,768]{1,0:T(8,128)} %get-tuple-element.47) | copy-start | bytes 884740
  170.2 5.7 %copy-start = (bf16[1024,768]{1,0:T(8,128)(2,1)S(1)}, bf16[1024,768]{1,0:T(8,128)(2,1)}, u32[]{:S(2)}) copy-start(bf16[1024,768]{1,0:T(8,128)(2,1)} %get-tuple-element.32) | copy-start | bytes 4718596
  175.9 2.0 %copy-start.1 = (bf16[32,32,768]{2,1,0:T(8,128)(2,1)S(1)}, bf16[32,32,768]{2,1,0:T(8,128)(2,1)}, u32[]{:S(2)}) copy-start(bf16[32,32,768]{2,1,0:T(8,128)(2,1)} %get-tuple-element.46) | copy-start | bytes 4718596
